TPU v7x, 32 devices: a whole 2x2x4 slice. The times are simulated.
32 devices in a mesh: dp: 2 (over y), seq: 4 (over x, core), tensor: 4 (over z).
Axes of the slice: x: 2, y: 2, z: 4, core: 2. Of those that a mesh axis runs over, the one named last changes fastest.
Arguments:
- inputs: bfloat16 [6, 2048, 768], P('dp', 'seq'), may hold values from -6 to 6
- lengths: int32 [6], P('dp'), may hold values from 512 to 2048, as said below
- gain_attn: bfloat16 [768], P('dp'), may hold values from 0.5 to 1.5
- w_query: bfloat16 [768, 768], P('dp', 'tensor'), may hold values from -0.109375 to 0.109375
- w_key: bfloat16 [768, 768], P('dp', 'tensor'), may hold values from -0.109375 to 0.109375
- w_value: bfloat16 [768, 768], P('dp', 'tensor'), may hold values from -0.21875 to 0.21875
- w_out: bfloat16 [768, 768], P('tensor', 'dp'), may hold values from -1.75 to 1.75
- bias_table: bfloat16 [32, 12], P('dp', 'tensor'), may hold values from -4 to 4
- gain_ffn: bfloat16 [768], P('dp'), may hold values from 0.5 to 1.5
- w_in: bfloat16 [768, 3072], P('dp', 'tensor'), may hold values from -0.21875 to 0.21875
- w_down: bfloat16 [3072, 768], P('tensor', 'dp'), may hold values from -0.15625 to 0.15625
- cotangent: bfloat16 [6, 2048, 768], P('dp', 'seq'), may hold values from -6 to 6
Outputs:
- outputs: bfloat16 [6, 2048, 768], P('dp', 'seq')
- grad_inputs: bfloat16 [6, 2048, 768], P('dp', 'seq')
- grad_gain_attn: float32 [768], P('dp')
- grad_query: float32 [768, 768], P('dp', 'tensor')
- grad_key: float32 [768, 768], P('dp', 'tensor')
- grad_value: float32 [768, 768], P('dp', 'tensor')
- grad_out: float32 [768, 768], P('tensor', 'dp')
- grad_table: float32 [32, 12], P('dp', 'tensor')
- grad_gain_ffn: float32 [768], P('dp')
- grad_in: float32 [768, 3072], P('dp', 'tensor')
- grad_down: float32 [3072, 768], P('tensor', 'dp')
Inputs may be any that keep to these rules, and one draw needn't show every extreme that they name: `lengths`: real tokens of each sequence, counted from its first slot; in every draw some sequence fills all 2048 slots.
All inputs are finite; a program needn't handle non-finite values.
Results may differ from a plain program's by a relative error of at most 0.019.
Values may be sent and summed in bfloat16 or wider, within the bound.
No kernel may reach another device: no remote copies, remote signals or barrier semaphores. Data moves between devices by JAX's collectives and lax.ppermute only.
A program may use at most 256 MiB of HBM per device.

v0:
```python
import functools

import jax
import jax.numpy as jnp
from jax import lax
from jax.experimental import pallas as pl
from jax.experimental.pallas import tpu as pltpu
from jax.sharding import PartitionSpec as P

HEAD = 64
BUCKETS = 32
EPSILON = 1e-06
LIMITS = (12, 16, 23, 32, 46, 64, 91)
LOW = jnp.bfloat16
FULL = jnp.float32
TILE = 128
RANKS = 4
MIX = (0, 2, 1, 3)
IDLE = 1
SPLIT = 2
EXTRA = 32
SHORTEN = 64
GELU_A = 0.7978845608028654
GELU_B = 0.044715
KERNEL_MEMORY = 60 * 1024 * 1024


def bucket_of(relative):
    sign_part = jnp.where(relative > 0, 16, 0).astype(jnp.int32)
    distance = jnp.abs(relative)
    far_part = jnp.full(distance.shape, 8, jnp.int32)
    for limit in LIMITS:
        far_part = far_part + (distance >= limit).astype(jnp.int32)
    return sign_part + jnp.where(distance < 8, distance, far_part)


def dot_nn(left, right):
    return lax.dot_general(left, right, (((1,), (0,)), ((), ())), preferred_element_type=FULL)


def dot_nt(left, right):
    return lax.dot_general(left, right, (((1,), (1,)), ((), ())), preferred_element_type=FULL)


def dot_tn(left, right):
    return lax.dot_general(left, right, (((0,), (0,)), ((), ())), preferred_element_type=FULL)


def tile_place(tile, per):
    sub = per // SPLIT
    return ((tile % per) // sub) * (RANKS * sub) + (tile // per) * sub + tile % sub


def tile_at(place, per):
    sub = per // SPLIT
    return ((place // sub) % RANKS) * per + (place // (RANKS * sub)) * sub + place % sub


def cost(flops):
    return pl.CostEstimate(flops=flops // SHORTEN, bytes_accessed=0, transcendentals=0)


def params():
    return pltpu.CompilerParams(vmem_limit_bytes=KERNEL_MEMORY)


def whole_spec(shape):
    return pl.BlockSpec(shape, lambda i, c: tuple(0 for _ in shape))


def near_bucket(d):
    key = lax.broadcasted_iota(jnp.int32, (TILE, TILE), 0)
    query = lax.broadcasted_iota(jnp.int32, (TILE, TILE), 1)
    return bucket_of(TILE * d + key - query)


def buckets_near(d):
    half = BUCKETS // 2
    if d < 0:
        return range(half)
    return range(half, BUCKETS) if d > 0 else range(BUCKETS)


def pick_block(index, refs):
    value = refs[0][...]
    for k in range(1, len(refs)):
        value = jnp.where(index == k, refs[k][...], value)
    return value


def pick_pair(info, chunk, refs):
    return jnp.concatenate([pick_block(info[chunk + k], refs) for k in range(2)], axis=0)


def project_kernel(
    heads, per, info, x0, x1, x2, x3, gain_ref, w_ref, table, normed, qa, ka, va, kt, vt, near
):
    step = pl.program_id(0)

    @pl.when(step == 0)
    def _():
        for d in (-1, 0, 1):
            buckets = near_bucket(d)
            for h in range(heads):
                tile = jnp.zeros((TILE, TILE), FULL)
                for b in buckets_near(d):
                    tile = jnp.where(buckets == b, table[b, h], tile)
                near[h, d + 1] = tile

    rows = 2 * x0.shape[0]
    x = pick_pair(info, (2 * step) % RANKS, (x0, x1, x2, x3)).astype(FULL)
    scale = lax.rsqrt(jnp.mean(x * x, axis=-1, keepdims=True) + EPSILON)
    xn = (x * scale * gain_ref[...]).astype(LOW)
    normed[...] = xn
    y = dot_nt(xn, w_ref[...])
    row = lax.broadcasted_iota(jnp.int32, (rows, TILE), 0)
    lane = lax.broadcasted_iota(jnp.int32, (rows, TILE), 1) - HEAD
    place = step * (rows // TILE) + row // TILE
    count = RANKS * per
    is_tile = jnp.logical_and(lane >= 0, lane < count)
    here = tile_at(place, per)
    there = tile_at(jnp.where(is_tile, lane, 0), per)
    position = here * TILE + row % TILE
    q_extra = jnp.where(jnp.logical_or(lane == place, lane == count), 1.0, 0.0)
    v_extra = jnp.where(lane == 0, 1.0, 0.0)
    dead = jnp.where(jnp.logical_and(lane == count, position >= info[RANKS]), -1e30, 0.0)
    left = jnp.logical_and(is_tile, here < there - 1)
    right = jnp.logical_and(is_tile, here > there + 1)
    wide = heads * TILE
    for h in range(heads):
        before, behind = table[BUCKETS // 2 - 1, h], table[BUCKETS - 1, h]
        k_extra = jnp.where(left, before, jnp.where(right, behind, dead))
        at = slice(TILE * h, TILE * h + TILE)
        qa[:, at] = (y[:, at] + q_extra).astype(LOW)
        kh = y[:, wide + TILE * h : wide + TILE * h + TILE] + k_extra
        vh = y[:, 2 * wide + TILE * h : 2 * wide + TILE * h + TILE] + v_extra
        ka[:, at] = kh.astype(LOW)
        va[:, at] = vh.astype(LOW)
        kt[at, :] = kh.T.astype(LOW)
        vt[at, :] = vh.T.astype(LOW)


def project(info, xs, gain, w_qkv, table, heads, per):
    total = RANKS * xs[0].shape[0]
    rows = xs[0].shape[0] // SPLIT
    width = xs[0].shape[1]
    row_block = lambda w: pl.BlockSpec((2 * rows, w), lambda i, c: (i, 0))
    col_block = lambda w: pl.BlockSpec((w, 2 * rows), lambda i, c: (0, i))
    wide = heads * TILE
    return pl.pallas_call(
        functools.partial(project_kernel, heads, per),
        grid_spec=pltpu.PrefetchScalarGridSpec(
            num_scalar_prefetch=1,
            grid=(RANKS * SPLIT // 2,),
            in_specs=[pl.BlockSpec((rows, width), lambda i, c: (2 * i // RANKS, 0))] * RANKS
            + [
                whole_spec(gain.shape),
                whole_spec(w_qkv.shape),
                pl.BlockSpec(memory_space=pltpu.SMEM),
            ],
            out_specs=[
                row_block(width),
                row_block(wide),
                row_block(wide),
                row_block(wide),
                col_block(wide),
                col_block(wide),
                whole_spec((heads, 3, TILE, TILE)),
            ],
        ),
        out_shape=[
            jax.ShapeDtypeStruct((total, width), LOW),
            jax.ShapeDtypeStruct((total, wide), LOW),
            jax.ShapeDtypeStruct((total, wide), LOW),
            jax.ShapeDtypeStruct((total, wide), LOW),
            jax.ShapeDtypeStruct((wide, total), LOW),
            jax.ShapeDtypeStruct((wide, total), LOW),
            jax.ShapeDtypeStruct((heads, 3, TILE, TILE), FULL),
        ],
        compiler_params=params(),
        name="project",
        cost_estimate=cost(8 * total * width * heads * HEAD),
    )(info, *xs, gain, w_qkv, table)


def near_tiles(first_place, tiles, per, visit):
    count = RANKS * per
    for u in range(tiles):
        here = tile_at(first_place + u, per)
        for d in (-1, 0, 1):
            there = here + d
            valid = jnp.logical_and(there >= 0, there < count)
            place = tile_place(jnp.clip(there, 0, count - 1), per)
            rows = pl.ds(pl.multiple_of(place * TILE, TILE), TILE)
            visit(d + 1, rows, slice(u * TILE, u * TILE + TILE), jnp.where(valid, 1.0, 0.0))


def score_block(h, first_place, per, qa, ka, near, s_ref):
    bq = qa.shape[0]
    at = slice(TILE * h, TILE * h + TILE)
    s_ref[h] = dot_nt(ka[:, at], qa[:, at])

    def add(d, rows, cols, valid):
        s_ref[h, rows, cols] = s_ref[h, rows, cols] + near[h, d] * valid

    near_tiles(first_place, bq // TILE, per, add)


def forward_kernel(heads, per, offset, qa, ka, vt, near, mixed, ot, lse, s_ref):
    bq = qa.shape[0]
    first = (pl.program_id(0) + offset) * (bq // TILE)
    for h in range(heads):
        score_block(h, first, per, qa, ka, near, s_ref)
    parts = []
    for h in range(heads):
        s = s_ref[h]
        top = jnp.max(s, axis=0, keepdims=True)
        p = jnp.exp(s - top).astype(LOW)
        o = dot_nn(vt[TILE * h : TILE * h + TILE, :], p)
        total = o[HEAD : HEAD + 1]
        o = o[:HEAD] * (1.0 / total)
        ot[HEAD * h : HEAD * h + HEAD, :] = o
        lse[h : h + 1, :] = top + jnp.log(total)
        parts.append(o.T)
    mixed[...] = jnp.concatenate(parts, axis=1).astype(LOW)


def attend(qa, ka, vt, near, part, bq, per):
    total, wide = ka.shape
    heads = wide // TILE
    span = total // SPLIT
    steps = span // bq
    offset = part * steps
    full = lambda shape: pl.BlockSpec(shape, lambda i: tuple(0 for _ in shape))
    width = heads * HEAD
    return pl.pallas_call(
        functools.partial(forward_kernel, heads, per, offset),
        grid=(steps,),
        in_specs=[
            pl.BlockSpec((bq, wide), lambda i: (i + offset, 0)),
            full(ka.shape),
            full(vt.shape),
            full(near.shape),
        ],
        out_specs=[
            pl.BlockSpec((bq, width), lambda i: (i, 0)),
            pl.BlockSpec((width, bq), lambda i: (0, i)),
            pl.BlockSpec((8, bq), lambda i: (0, i)),
        ],
        out_shape=[
            jax.ShapeDtypeStruct((span, width), LOW),
            jax.ShapeDtypeStruct((width, span), FULL),
            jax.ShapeDtypeStruct((8, span), FULL),
        ],
        scratch_shapes=[pltpu.VMEM((heads, total, bq), FULL)],
        compiler_params=params(),
        name="attend",
        cost_estimate=cost(20 * heads * span * total * HEAD),
    )(qa, ka, vt, near)


def middle_kernel(
    first, info, x0, x1, x2, x3, c0, c1, c2, c3, m0, m1, m2, m3, w0, w1, w2, w3,
    gain, w_ffn, *refs
):
    given, (f_keep, f_give, d_keep, d_give, resid_out, grads_out, grads) = refs[:-7], refs[-7:]
    step = pl.program_id(0)
    hid = w_ffn.shape[1] // 2

    @pl.when(step == 0)
    def _():
        grads[...] = jnp.zeros_like(grads) if first else given[0][...].astype(FULL)

    attn = dot_nn(m0[...], w0[...]) + dot_nn(m1[...], w1[...])
    attn = attn + dot_nn(m2[...], w2[...]) + dot_nn(m3[...], w3[...])
    resid = pick_block(info[step], (x0, x1, x2, x3)).astype(FULL) + attn
    resid_out[...] = resid
    scale = lax.rsqrt(jnp.mean(resid * resid, axis=-1, keepdims=True) + EPSILON)
    normed = (resid * scale * gain[...]).astype(LOW)
    hidden = dot_nn(normed, w_ffn[:, :hid])
    grad = pick_block(info[step], (c0, c1, c2, c3))
    d_active = dot_nn(grad, w_ffn[:, hid:])
    square = hidden * hidden
    th = jnp.tanh(GELU_A * hidden * (1.0 + GELU_B * square))
    half = 0.5 * (1.0 + th)
    active = (hidden * half).astype(LOW)
    slope = half + 0.5 * hidden * (1.0 - th * th) * (GELU_A * (1.0 + (3.0 * GELU_B) * square))
    d_hidden = (d_active * slope).astype(LOW)
    dn = dot_nt(d_hidden, w_ffn[:, :hid]).astype(LOW)
    ffn = dot_nt(active, w_ffn[:, hid:]).astype(LOW)

    @pl.when(info[step] % 2 == 0)
    def _():
        d_keep[0] = dn
        f_keep[0] = ffn

    @pl.when(info[step] % 2 == 1)
    def _():
        d_give[0] = dn
        f_give[0] = ffn

    grads[:, :hid] += dot_tn(normed, d_hidden)
    grads[:, hid:] += dot_tn(grad, active)

    @pl.when(step == RANKS - 1)
    def _():
        grads_out[...] = grads[...].astype(LOW)


def middle(info, xs, cs, pieces, outs, gain, w_ffn, part, given):
    rows, width = xs[0].shape[0] // SPLIT, xs[0].shape[1]
    narrow = pieces[0].shape[1]
    own_block = pl.BlockSpec((rows, width), lambda i, c: (part, 0))
    piece_block = pl.BlockSpec((rows, narrow), lambda i, c: (i, 0))
    rel_block = pl.BlockSpec((1, rows, width), lambda i, c: (c[i] // 2, 0, 0))
    pair_block = pl.BlockSpec((1, rows, width), lambda i, c: (i // 2, 0, 0))
    extra = () if given is None else (given,)
    two = jax.ShapeDtypeStruct((2, rows, width), LOW)
    return pl.pallas_call(
        functools.partial(middle_kernel, given is None),
        grid_spec=pltpu.PrefetchScalarGridSpec(
            num_scalar_prefetch=1,
            grid=(RANKS,),
            in_specs=[own_block] * (2 * RANKS)
            + [piece_block] * RANKS
            + [whole_spec(outs[0].shape)] * RANKS
            + [whole_spec(v.shape) for v in (gain, w_ffn) + extra],
            out_specs=[
                rel_block,
                rel_block,
                pair_block,
                pair_block,
                pl.BlockSpec((rows, width), lambda i, c: (i, 0)),
                whole_spec(w_ffn.shape),
            ],
            scratch_shapes=[pltpu.VMEM(w_ffn.shape, FULL)],
        ),
        out_shape=[two, two, two, two]
        + [
            jax.ShapeDtypeStruct((RANKS * rows, width), FULL),
            jax.ShapeDtypeStruct(w_ffn.shape, LOW),
        ],
        compiler_params=params(),
        name="middle",
        cost_estimate=cost(20 * RANKS * rows * width * w_ffn.shape[1] // 2),
    )(info, *xs, *cs, *pieces, *outs, gain, w_ffn, *extra)


def backward_kernel(
    per, offset, kc, info, qa, ka, kt, va, sum_mine, sum_other, resid_ref,
    c0, c1, c2, c3, gain, wo, ot, lse, near, *refs
):
    given = refs[:-11]
    dq, dk, dv, d_near, g_out, tiles, s_ref, ds_ref, dk_acc, dv_acc, d_rows = refs[-11:]
    head, step = pl.program_id(0), pl.program_id(1)
    bq = qa.shape[0]
    total = ka.shape[0]
    count = RANKS * per
    first = (step + offset) * (bq // TILE)
    here = pl.ds(pl.multiple_of(step * bq, bq), bq)

    @pl.when(step == 0)
    def _():
        if len(given) > 0:
            dk_acc[...] = given[0][...]
            dv_acc[...] = given[1][...]
            d_near[...] = given[2][...]
            g_out[...] = given[3][...]
        else:
            dk_acc[...] = jnp.zeros_like(dk_acc)
            dv_acc[...] = jnp.zeros_like(dv_acc)
            d_near[...] = jnp.zeros_like(d_near)
            g_out[...] = jnp.zeros_like(g_out)

    @pl.when(head == 0)
    def _():
        even = info[2 * step] % 2 == 0
        mine, other = sum_mine[0], sum_other[0]
        d_norm = jnp.concatenate(
            [jnp.where(even, mine, other), jnp.where(even, other, mine)], axis=0
        ).astype(FULL)
        cot = jnp.concatenate(
            [pick_block(info[2 * step + k], (c0, c1, c2, c3)) for k in range(2)], axis=0
        ).astype(FULL)
        resid = resid_ref[...]
        scale = lax.rsqrt(jnp.mean(resid * resid, axis=-1, keepdims=True) + EPSILON)
        unit = resid * scale
        along = d_norm * gain[...]
        rows = cot + scale * (along - unit * jnp.mean(along * unit, axis=-1, keepdims=True))
        d_rows[here, :] = rows.astype(LOW)

    s_ref[...] = dot_nt(ka[...], qa[...])

    def add(d, rows, cols, valid):
        s_ref[rows, cols] = s_ref[rows, cols] + near[0, d] * valid

    near_tiles(first, bq // TILE, per, add)
    grad = d_rows[here, :]
    do = dot_nt(grad, wo[...]).astype(LOW)
    do_t = dot_nt(wo[...], grad).astype(LOW).astype(FULL)
    o_t = ot[...]
    g_out[...] += dot_nn(o_t.astype(LOW), grad)
    delta = jnp.sum(do_t[:HEAD] * o_t, axis=0, keepdims=True)
    lse_row = lse[pl.ds(head, 1), :]
    dq_t = jnp.zeros((TILE, bq), FULL)
    for c in range(total // kc):
        rows = slice(kc * c, kc * c + kc)
        p = jnp.exp(s_ref[rows, :] - lse_row)
        d_p = dot_nt(va[rows, :], do)
        d_s = (p * (d_p - delta)).astype(LOW)
        ds_ref[rows, :] = d_s
        dv_acc[rows, :] += dot_nn(p.astype(LOW), do)
        dk_acc[rows, :] += dot_nn(d_s, qa[...])
        dq_t += dot_nn(kt[:, rows], d_s)
    lane = lax.broadcasted_iota(jnp.int32, (bq, TILE), 1)
    dq[...] = jnp.where(lane < HEAD, dq_t.T, 0.0).astype(LOW)

    def collect(d, rows, cols, valid):
        d_near[0, d] += ds_ref[rows, cols].astype(FULL) * valid

    near_tiles(first, bq // TILE, per, collect)

    @pl.when(step == pl.num_programs(1) - 1)
    def _():
        if dk.dtype == FULL:
            dk[...] = dk_acc[...]
            dv[...] = dv_acc[...]
        else:
            side = lax.broadcasted_iota(jnp.int32, (total, TILE), 1)
            dk[...] = jnp.where(side < HEAD, dk_acc[...], 0.0).astype(LOW)
            dv[...] = jnp.where(side < HEAD, dv_acc[...], 0.0).astype(LOW)
        sums = [
            jnp.sum(dk_acc[k * TILE : k * TILE + TILE, :], axis=0, keepdims=True)
            for k in range(count)
        ]
        tiles[0] = jnp.concatenate(sums, axis=0)


def attend_back(
    info, qa, ka, kt, va, sums, resid, cs, gain, wo, ot, lse, near, part, kc, per, given
):
    total, wide = ka.shape
    heads = wide // TILE
    model = resid.shape[1]
    rows = total // SPLIT // RANKS
    bq = 2 * rows
    span = total // SPLIT
    steps = span // bq
    offset = part * steps
    last = part == SPLIT - 1
    once = lambda h, i: jnp.where(h == 0, i, steps - 1)
    head_cols = pl.BlockSpec((total, TILE), lambda h, i, c: (0, h))
    near_block = pl.BlockSpec((1, 3, TILE, TILE), lambda h, i, c: (h, 0, 0, 0))
    out_block = pl.BlockSpec((HEAD, model), lambda h, i, c: (h, 0))
    kind = LOW if last else FULL
    full = lambda shape: pl.BlockSpec(shape, lambda h, i, c: tuple(0 for _ in shape))
    return pl.pallas_call(
        functools.partial(backward_kernel, per, offset, kc),
        grid_spec=pltpu.PrefetchScalarGridSpec(
            num_scalar_prefetch=1,
            grid=(heads, steps),
            in_specs=[
                pl.BlockSpec((bq, TILE), lambda h, i, c: (i + offset, h)),
                head_cols,
                pl.BlockSpec((TILE, total), lambda h, i, c: (h, 0)),
                head_cols,
            ]
            + [pl.BlockSpec((1, rows, model), lambda h, i, c: (once(h, i), 0, 0))] * 2
            + [pl.BlockSpec((bq, model), lambda h, i, c: (once(h, i), 0))]
            + [pl.BlockSpec((rows, model), lambda h, i, c: (part, 0))] * RANKS
            + [
                full(gain.shape),
                pl.BlockSpec((TILE, model), lambda h, i, c: (h, 0)),
                pl.BlockSpec((HEAD, bq), lambda h, i, c: (h, i)),
                pl.BlockSpec((8, bq), lambda h, i, c: (0, i)),
                near_block,
            ]
            + ([] if len(given) == 0 else [head_cols, head_cols, near_block, out_block]),
            out_specs=[
                pl.BlockSpec((bq, TILE), lambda h, i, c: (i, h)),
                head_cols,
                head_cols,
                near_block,
                out_block,
                pl.BlockSpec((1, RANKS * per, TILE), lambda h, i, c: (h, 0, 0)),
            ],
            scratch_shapes=[
                pltpu.VMEM((total, bq), FULL),
                pltpu.VMEM((total, bq), LOW),
                pltpu.VMEM((total, TILE), FULL),
                pltpu.VMEM((total, TILE), FULL),
                pltpu.VMEM((span, model), LOW),
            ],
        ),
        out_shape=[
            jax.ShapeDtypeStruct((span, wide), LOW),
            jax.ShapeDtypeStruct((total, wide), kind),
            jax.ShapeDtypeStruct((total, wide), kind),
            jax.ShapeDtypeStruct((heads, 3, TILE, TILE), FULL),
            jax.ShapeDtypeStruct((heads * HEAD, model), FULL),
            jax.ShapeDtypeStruct((heads, RANKS * per, TILE), FULL),
        ],
        compiler_params=params(),
        name="attend_back",
        cost_estimate=cost(40 * heads * span * total * HEAD),
    )(info, qa, ka, kt, va, *sums, resid, *cs, gain, wo, ot, lse, near, *given)


def bucket_kernel(d_near, out):
    heads = d_near.shape[0]
    found = [[jnp.zeros((1, TILE), FULL)] * BUCKETS for _ in range(heads)]
    for d in (-1, 0, 1):
        buckets = near_bucket(d)
        for b in buckets_near(d):
            here = buckets == b
            for h in range(heads):
                found[h][b] = found[h][b] + jnp.sum(
                    jnp.where(here, d_near[h, d + 1], 0.0), axis=0, keepdims=True
                )
    for h in range(heads):
        out[h] = jnp.concatenate(found[h], axis=0)


def bucket_sums(d_near):
    heads = d_near.shape[0]
    return pl.pallas_call(
        bucket_kernel,
        out_shape=jax.ShapeDtypeStruct((heads, BUCKETS, TILE), FULL),
        compiler_params=params(),
        name="bucket_sums",
    )(d_near)


def tail_kernel(info, dq0, dq1, dk, dv, w_ref, keep, give):
    wide = dk.shape[1]
    dq = pick_block(pl.program_id(0), (dq0, dq1))
    out = dot_nn(dq, w_ref[:wide, :]) + dot_nn(dk[...], w_ref[wide : 2 * wide, :])
    out = (out + dot_nn(dv[...], w_ref[2 * wide :, :])).astype(LOW)
    rows = out.shape[0] // RANKS
    even = info[0] % 2 == 0
    low = info[0] // 2 == 0
    parts = [out[k * rows : k * rows + rows] for k in range(RANKS)]
    kept = [jnp.where(even, parts[k], parts[k + 1]) for k in (0, 2)]
    given = [jnp.where(even, parts[k + 1], parts[k]) for k in (0, 2)]
    keep[0], keep[1] = jnp.where(low, kept[0], kept[1]), jnp.where(low, kept[1], kept[0])
    give[0], give[1] = jnp.where(low, given[0], given[1]), jnp.where(low, given[1], given[0])


def tail(info, dqs, dk, dv, w_wide):
    total, wide = dk.shape
    model = w_wide.shape[1]
    span = total // SPLIT
    rows = span // RANKS
    rel_block = pl.BlockSpec((2, rows, model), lambda i, c: (i, 0, 0))
    return pl.pallas_call(
        tail_kernel,
        grid_spec=pltpu.PrefetchScalarGridSpec(
            num_scalar_prefetch=1,
            grid=(SPLIT,),
            in_specs=[
                whole_spec((span, wide)),
                whole_spec((span, wide)),
                pl.BlockSpec((span, wide), lambda i, c: (i, 0)),
                pl.BlockSpec((span, wide), lambda i, c: (i, 0)),
                whole_spec(w_wide.shape),
            ],
            out_specs=[rel_block, rel_block],
        ),
        out_shape=[jax.ShapeDtypeStruct((2 * SPLIT, rows, model), LOW)] * 2,
        compiler_params=params(),
        name="tail",
        cost_estimate=cost(6 * total * wide * model),
    )(info, *dqs, dk, dv, w_wide)


def weights_kernel(steps, dq0, dq1, dk, dv, normed, g_out, extra, out, acc):
    step = pl.program_id(0)

    @pl.when(step == 0)
    def _():
        acc[...] = jnp.zeros_like(acc)

    dq = pick_block(step // (steps // 2), (dq0, dq1))
    acc[...] += dot_tn(jnp.concatenate([dq, dk[...], dv[...]], axis=1), normed[...])

    @pl.when(step == steps - 1)
    def _():
        count = acc.shape[0] // TILE
        for j in range(count):
            out[j * HEAD : j * HEAD + HEAD, :] = acc[j * TILE : j * TILE + HEAD, :].astype(LOW)
        base = count * HEAD
        out[base : base + g_out.shape[0], :] = g_out[...].astype(LOW)
        out[base + g_out.shape[0] :, :] = extra[...]


def weights(dqs, dk, dv, normed, g_out, extra):
    total, wide = dk.shape
    model = normed.shape[1]
    steps = 4
    rows = total // steps
    half = steps // 2
    full = lambda shape: pl.BlockSpec(shape, lambda i: tuple(0 for _ in shape))
    block = lambda w: pl.BlockSpec((rows, w), lambda i: (i, 0))
    out_rows = 3 * wide * HEAD // TILE + g_out.shape[0] + extra.shape[0]
    return pl.pallas_call(
        functools.partial(weights_kernel, steps),
        grid=(steps,),
        in_specs=[
            pl.BlockSpec((rows, wide), lambda i: (jnp.minimum(i, half - 1), 0)),
            pl.BlockSpec((rows, wide), lambda i: (jnp.maximum(i - half, 0), 0)),
            block(wide),
            block(wide),
            block(model),
            full(g_out.shape),
            full(extra.shape),
        ],
        out_specs=full((out_rows, model)),
        out_shape=jax.ShapeDtypeStruct((out_rows, model), LOW),
        scratch_shapes=[pltpu.VMEM((3 * wide, model), FULL)],
        compiler_params=params(),
        name="weights",
        cost_estimate=cost(6 * total * wide * model),
    )(*dqs, dk, dv, normed, g_out, extra)


def together(*values):
    return lax.optimization_barrier(values)


def after(value, *given):
    return lax.optimization_barrier((value,) + given)[0]


def swap_seq(value, bit):
    return lax.ppermute(value, "seq", [(i, i ^ bit) for i in range(RANKS)])


def regroup(value, skip):
    pairs = []
    for s in range(RANKS):
        for t in range(RANKS):
            if t != skip and MIX[s] != 0:
                pairs.append((s * RANKS + t, s * RANKS + (t ^ MIX[s])))
    moved = lax.ppermute(value, ("seq", "tensor"), pairs)
    return jnp.where(lax.axis_index("seq") == MIX.index(0), value, moved)


def along_tensor(value, pairs):
    return lax.ppermute(value, "tensor", pairs)


def step_one(own):
    return along_tensor(own, [(0, 1), (2, 3)]), along_tensor(own, [(3, 2), (2, 1)])


def step_two(moved):
    return along_tensor(moved[0], [(1, 2)]), along_tensor(moved[1], [(2, 1), (1, 0)])


def step_three(moved):
    return along_tensor(moved[0], [(2, 3)]), along_tensor(moved[1], [(1, 0)])


HOME = (0, 0, 1, 2)
PLACES = (
    ((None, 0, None, 1), (None, 1, 2, None)),
    ((None, None, 0, None), (1, 2, None, None)),
    ((None, None, None, 0), (2, None, None, None)),
)


def by_rank(values, rank):
    out = values[0]
    for index in range(1, len(values)):
        out = jnp.where(rank == index, values[index], out)
    return out


def keep_step(held, own, moved, places, rank):
    for value, place in zip(moved, places):
        got = by_rank([p is not None for p in place], rank)
        at = by_rank([HOME[k] if p is None else p for k, p in enumerate(place)], rank)
        value = jnp.where(got, value, own)
        held = lax.dynamic_update_slice(held, value[None], (at, 0, 0))
    return held


def swap_dp(value):
    return lax.ppermute(value, "dp", [(0, 1), (1, 0)])


def join_dp(halves, axis):
    if len(halves) == 1:
        return lax.all_gather(halves[0], "dp", axis=axis, tiled=True)
    value, other = halves
    swap = lax.axis_index("dp") == 1
    return jnp.concatenate(
        [jnp.where(swap, other, value), jnp.where(swap, value, other)], axis=axis
    )


def gather_dp(value, axis):
    if lax.axis_size("dp") != 2:
        return join_dp((value,), axis)
    return join_dp((value, swap_dp(value)), axis)


def scatter_dp(value, axis):
    if lax.axis_size("dp") != 2:
        return lax.psum_scatter(value, "dp", scatter_dimension=axis, tiled=True).astype(LOW)
    size = value.shape[axis] // 2
    mine = lax.axis_index("dp")
    keep = lax.dynamic_slice_in_dim(value, mine * size, size, axis)
    give = lax.dynamic_slice_in_dim(value, (1 - mine) * size, size, axis)
    return (keep.astype(FULL) + swap_dp(give.astype(LOW)).astype(FULL)).astype(LOW)


def sum_pair(value, bit):
    return value.astype(FULL) + swap_seq(value, bit).astype(FULL)


def normalize(values):
    scale = lax.rsqrt(jnp.mean(values * values, axis=-1, keepdims=True) + EPSILON)
    return values * scale, scale


def norm_back(grad, unit, scale, gain):
    along = grad * gain
    return scale * (along - unit * jnp.mean(along * unit, axis=-1, keepdims=True))


def body(
    inputs, lengths, gain_attn, w_query, w_key, w_value, w_out, bias_table,
    gain_ffn, w_in, w_down, cotangent,
):
    slots, rows_here, model = inputs.shape
    assert lax.axis_size("seq") == RANKS and lax.axis_size("tensor") == RANKS and slots == 3
    total = RANKS * rows_here
    per = rows_here // TILE
    narrow = w_query.shape[1]
    heads = narrow // HEAD
    hid = w_in.shape[1]
    rank = lax.axis_index("tensor")
    chunk = lax.axis_index("seq")
    mine = lax.axis_index("dp")
    slot = jnp.where(rank == 0, 0, rank - 1)
    length = lax.dynamic_index_in_dim(lengths, slot, 0, keepdims=False)
    order = jnp.bitwise_xor(chunk, jnp.arange(RANKS, dtype=jnp.int32)).astype(jnp.int32)
    info = jnp.concatenate([order, length[None], jnp.zeros((3,), jnp.int32)])
    rows_part = rows_here // SPLIT
    size = gain_attn.shape[0]
    cut = lambda v: v.reshape(SPLIT, rows_part, model)

    x_own = lax.dynamic_index_in_dim(inputs, slot, 0, keepdims=False)
    x_far = swap_seq(x_own, 2)
    x_near = swap_seq(x_own, 1)

    flat = bias_table.reshape(-1)
    small = jnp.stack(
        [gain_attn, gain_ffn, jnp.pad(flat, (0, size - flat.shape[0]))]
        + [jnp.zeros((size,), LOW)] * (EXTRA - 3)
    )
    w_first = after(w_query, x_own)
    pack = jnp.concatenate([w_first.T, w_key.T, w_value.T, w_out, small], axis=0)
    pack = regroup(pack, None)
    w_all = gather_dp(pack, 1)
    main = 4 * narrow
    w_wide = jnp.pad(
        w_all[: 3 * narrow].reshape(3 * heads, HEAD, model), ((0, 0), (0, TILE - HEAD), (0, 0))
    ).reshape(3 * heads * TILE, model)
    gain_one = w_all[main : main + 1].astype(FULL)
    gain_two = w_all[main + 1 : main + 2].astype(FULL)
    table = w_all[main + 2].reshape(-1, size)[:, : flat.shape[0]]
    table = table.reshape(BUCKETS, heads).astype(FULL)
    xs = [x_own, x_near, x_far, swap_seq(x_far, 1)]

    position = chunk * rows_here + jnp.arange(rows_here, dtype=jnp.int32)
    live = jnp.logical_and(position < length, rank != IDLE)
    c_own = lax.dynamic_index_in_dim(cotangent, slot, 0, keepdims=False)
    c_own = jnp.where(live[:, None], c_own, jnp.zeros((), LOW))
    ffn_pack = regroup(after(jnp.concatenate([w_in, w_down.T], axis=1), pack), None)
    c_first = after(c_own, x_far)
    c_far = swap_seq(c_first, 2)

    normed, qa, ka, va, kt, vt, near = project(info, xs, gain_one, w_wide, table, heads, per)

    normed, c_far, ffn_pack = together(normed, c_far, ffn_pack)
    qa, ka, vt, _ = together(qa, ka, vt, normed)
    out_mine = w_all[3 * narrow : main]
    out_near, out_far = swap_seq(out_mine, 1), swap_seq(out_mine, 2)
    ffn_halves = (ffn_pack, swap_dp(ffn_pack)) if lax.axis_size("dp") == 2 else (ffn_pack,)
    cs = [c_own, swap_seq(c_first, 1), c_far, swap_seq(c_far, 1)]
    out_wide = jnp.pad(
        out_mine.reshape(heads, HEAD, model), ((0, 0), (0, TILE - HEAD), (0, 0))
    ).reshape(heads * TILE, model)

    bq = min(1024, total // SPLIT)
    attended = [attend(qa, ka, vt, near, 0, bq, per)]
    attended[0], cs, out_far = together(attended[0], cs, out_far)
    outs = [out_mine, out_near, out_far, swap_seq(out_far, 1)]
    mixed = attended[0][0]
    pieces = [[mixed] + [swap_seq(mixed, bit) for bit in (1, 2, 3)]]

    attended.append(attend(after(qa, mixed), ka, vt, near, 1, bq, per))
    attended[1], pieces[0], outs, ffn_halves = together(
        attended[1], pieces[0], outs, ffn_halves
    )
    w_ffn = join_dp(ffn_halves, 0)
    mixed = attended[1][0]
    pieces.append([mixed] + [swap_seq(mixed, bit) for bit in (1, 2, 3)])

    def chip_sum(mid, core):
        return (mid[2].astype(FULL) + core.astype(FULL)).astype(LOW)

    def whole_sum(part):
        both = chip[part].astype(FULL) + chip_far[part].astype(FULL)
        both = both.astype(LOW)
        return both, swap_seq(both, 1)

    def out_rows(part):
        resid = lax.dynamic_index_in_dim(
            mids[part][4].reshape(RANKS, rows_part, model), chunk, 0, keepdims=False
        )
        return (resid + (ffn[part][0] + ffn_far[part].astype(FULL))).astype(LOW)

    mids, chip, chip_far = [], [], []
    for part in range(SPLIT):
        mid = middle(
            info, xs, cs, pieces[part], outs, gain_two, w_ffn, part,
            None if part == 0 else mids[0][5],
        )
        if part == 0:
            mid, pieces[1] = together(mid, pieces[1])
        else:
            mid, chip_far[0] = together(mid, chip_far[0])
        mids.append(mid)
        chip.append(chip_sum(mid, swap_seq(mid[3], 1)))
        chip_far.append(swap_seq(chip[part], 2))
        if part == 0:
            pieces[1] = after(pieces[1], chip[0])

    sums = [whole_sum(0)]
    ffn = [after(mid[:2], chip[1]) for mid in mids]
    ffn = [f[0].astype(FULL) + swap_seq(f[1], 1).astype(FULL) for f in ffn]
    ffn_far = jnp.stack([f[1].astype(LOW) for f in ffn])
    g_ffn = after(mids[1][5], chip[1])
    g_ffn = lax.psum_scatter(g_ffn, "dp", scatter_dimension=0, tiled=True)
    sums[0] = after(sums[0], ffn_far)
    ffn_far = swap_seq(ffn_far, 2)

    args = (gain_two, out_wide)
    back = [
        attend_back(
            info, qa, ka, kt, va, sums[0], mids[0][4], cs, *args, *attended[0][1:], near, 0,
            512, per, (),
        )
    ]
    back[0], chip_far[1], ffn_far, g_ffn = together(back[0], chip_far[1], ffn_far, g_ffn)
    sums.append(whole_sum(1))
    out_own = jnp.concatenate([out_rows(part) for part in range(SPLIT)], axis=0)
    out_own = after(out_own, sums[1][0])
    g_ffn = regroup(g_ffn, IDLE)
    given = back[0][1:5]
    sums[1] = after(sums[1], out_own)
    back.append(
        attend_back(
            info, qa, ka, kt, va, sums[1], mids[1][4], cs, *args, *attended[1][1:], near, 1,
            512, per, given,
        )
    )
    back[1], g_ffn = together(back[1], g_ffn)
    outputs = lax.all_gather(after(out_own, g_ffn), "tensor")
    g_core = swap_seq(g_ffn, 1)
    dk, dv, d_near = back[1][1:4]
    resids = [
        lax.dynamic_index_in_dim(
            mid[4].reshape(RANKS, rows_part, model), chunk, 0, keepdims=False
        )
        for mid in mids
    ]

    dqs = [b[0] for b in back]
    keep, give = tail(info, dqs, dk, dv, w_wide)
    core = swap_seq(give, 1)
    found = bucket_sums(after(d_near, give))
    found, core, g_core = together(found, core, g_core)
    far_low = (keep[1::2].astype(FULL) + core[1::2].astype(FULL)).astype(LOW)
    far = swap_seq(far_low, 2)
    dqs, dk, dv, found, g_core = after((dqs, dk, dv, found, g_core), far_low)
    near_sum = jnp.sum(found, axis=2).T
    tile_sum = back[1][5][:, :, HEAD : HEAD + RANKS * per]
    tiles = tile_at(jnp.arange(RANKS * per), per)
    left = tiles[:, None] < tiles[None, :] - 1
    right = tiles[:, None] > tiles[None, :] + 1
    left_sum = jnp.sum(jnp.where(left, tile_sum, 0.0), axis=(1, 2))
    right_sum = jnp.sum(jnp.where(right, tile_sum, 0.0), axis=(1, 2))
    spot = jnp.arange(BUCKETS)[:, None]
    d_table = near_sum + jnp.where(spot == BUCKETS // 2 - 1, left_sum[None], 0.0)
    d_table = d_table + jnp.where(spot == BUCKETS - 1, right_sum[None], 0.0)
    d_table = d_table.reshape(model // size, flat.shape[0])
    d_table = jnp.pad(d_table, ((0, 0), (0, size - flat.shape[0]))).reshape(1, model)
    extra = jnp.concatenate([d_table, jnp.zeros((EXTRA - 1, model), FULL)], axis=0)
    g_all = weights(dqs, dk, dv, normed, back[1][4], extra.astype(LOW))
    g_all, far = together(g_all, far)
    x_parts, c_parts = cut(x_own).astype(FULL), cut(c_own).astype(FULL)
    own, gain_attn_part, gain_ffn_part = [], 0.0, 0.0
    for part in range(SPLIT):
        total_two = lax.dynamic_index_in_dim(sums[part][0], chunk // 2, 0, keepdims=False)
        total_two = total_two.astype(FULL)
        unit_two, scale_two = normalize(resids[part])
        gain_ffn_part = gain_ffn_part + jnp.sum(total_two * unit_two, axis=0)
        d_resid = c_parts[part] + norm_back(total_two, unit_two, scale_two, gain_two)
        unit, scale = normalize(x_parts[part])
        grad = keep[2 * part].astype(FULL) + core[2 * part].astype(FULL)
        grad = grad + far[part].astype(FULL)
        gain_attn_part = gain_attn_part + jnp.sum(grad * unit, axis=0)
        own.append((d_resid + norm_back(grad, unit, scale, gain_one)).astype(LOW))
    own = jnp.concatenate(own, axis=0)
    gains = jnp.stack([gain_attn_part, gain_ffn_part])
    g_ffn = (g_ffn.astype(FULL) + g_core.astype(FULL)).astype(LOW)
    g_all, g_ffn, gains = after((g_all, g_ffn, gains), own)

    held = jnp.zeros((slots, rows_here, model), LOW)
    home = by_rank(HOME, rank)
    held = lax.dynamic_update_slice(held, own[None], (home, 0, 0))
    one = step_one(own)
    gains = sum_pair(sum_pair(gains, 1), 2)
    g_all = scatter_dp(g_all, 1)
    g_far = swap_seq(after(g_ffn, gains), 2)
    one, g_all, gains, outputs = together(one, g_all, gains, outputs)

    two = step_two(one)
    held = keep_step(held, own, one, PLACES[0], rank)
    own = jnp.where(rank == IDLE, one[0], own)
    g_all = regroup(g_all, IDLE)
    gains = gains + swap_dp(gains) if lax.axis_size("dp") == 2 else lax.psum(gains, "dp")
    gains = gains + along_tensor(gains, [(t, t ^ 1) for t in range(RANKS)])
    g_ffn = g_ffn.astype(FULL) + g_far.astype(FULL)
    g_all = sum_pair(g_all, 1).astype(LOW)
    outputs = jnp.stack([outputs[0], outputs[2], outputs[3]])
    two, g_all, gains, held, g_ffn, outputs = together(two, g_all, gains, held, g_ffn, outputs)

    three = step_three(two)
    held = keep_step(held, own, two, PLACES[1], rank)
    g_all = sum_pair(g_all, 2)
    gains = gains + along_tensor(gains, [(t, t ^ 2) for t in range(RANKS)])
    grad_in, grad_down = g_ffn[:, :hid], g_ffn[:, hid:].T
    three, g_all, gains, held, grad_in, grad_down, outputs = together(
        three, g_all, gains, held, grad_in, grad_down, outputs
    )
    grad_inputs = keep_step(held, own, three, PLACES[2], rank)
    gains = lax.dynamic_slice_in_dim(gains, mine * size, size, 1)
    grad_gain_attn, grad_gain_ffn = gains[0], gains[1]
    grad_table = g_all[main, : flat.shape[0]].reshape(bias_table.shape)
    return (
        outputs,
        grad_inputs,
        grad_gain_attn,
        g_all[:narrow].T,
        g_all[narrow : 2 * narrow].T,
        g_all[2 * narrow : 3 * narrow].T,
        g_all[3 * narrow : main],
        grad_table,
        grad_gain_ffn,
        grad_in,
        grad_down,
    )


def solution(mesh):
    in_specs = (
        P("dp", "seq", None),
        P("dp"),
        P("dp"),
        P("dp", "tensor"),
        P("dp", "tensor"),
        P("dp", "tensor"),
        P("tensor", "dp"),
        P("dp", "tensor"),
        P("dp"),
        P("dp", "tensor"),
        P("tensor", "dp"),
        P("dp", "seq", None),
    )
    out_specs = (
        P("dp", "seq", None),
        P("dp", "seq", None),
        P("dp"),
        P("dp", "tensor"),
        P("dp", "tensor"),
        P("dp", "tensor"),
        P("tensor", "dp"),
        P("dp", "tensor"),
        P("dp"),
        P("dp", "tensor"),
        P("tensor", "dp"),
    )
    return jax.shard_map(body, mesh=mesh, in_specs=in_specs, out_specs=out_specs, check_vma=False)
```

profile of v0, /device:TPU:0, one launch (start us, length us, event | category | flops | bytes accessed | tf_op | source)
XLA Modules:
  0.0 413.7 jit_solution(11051290776459031726)
XLA Ops:
  7.3 2.3 dynamic-slice_bitcast_fusion
  10.4 1.5 collective-permute-start.3
  11.9 4.9 %collective-permute-start.1 = (bf16[512,768]{1,0:T(8,128)(2,1)}, bf16[512,768]{1,0:T(8,128)(2,1)}, u32[]{:S(2)}, u32[]{:S(2)}) collective-permute-start(bf16[512,768]{1,0:T(8,128)(2,1)} %get-tuple-element.377.x0), channel_id=1, source_target_pairs={{0,8},{4,12},{8,0},{12,4},{1,9},{5,13},{9,1},{13,5},{2,10},{6,14},... | collective-permute-start | bytes 2359304 | tf_op jit(solution)/shard_map/ppermute | solution.py:635
  19.4 1.6 collective-permute-start.4
  21.0 2.2 pad_maximum_fusion.2
  23.7 1.7 collective-permute-start.6
  26.0 2.2 bitcast_select_fusion
  28.2 6.5 %collective-permute-done.1.x2 = bf16[512,768]{1,0:T(8,128)(2,1)} collective-permute-done((bf16[512,768]{1,0:T(8,128)(2,1)}, bf16[512,768]{1,0:T(8,128)(2,1)}, u32[]{:S(2)}, u32[]{:S(2)}) %collective-permute-start.1) | collective-permute-done | bytes 786464 | tf_op jit(solution)/shard_map/ppermute | solution.py:635
  34.7 5.5 %collective-permute-start.2 = (bf16[512,768]{1,0:T(8,128)(2,1)}, bf16[512,768]{1,0:T(8,128)(2,1)}, u32[]{:S(2)}, u32[]{:S(2)}) collective-permute-start(bf16[512,768]{1,0:T(8,128)(2,1)} %collective-permute-done.1.x2), channel_id=1, source_target_pairs={{0,4},{4,0},{8,12},{12,8},{1,5},{5,1},{9,13},{13,9},{2,6},{6,2},{1... | collective-permute-start | bytes 2359304 | tf_op jit(solution)/shard_map/ppermute | solution.py:635
  41.5 4.9 %collective-permute-start.5 = (bf16[512,768]{1,0:T(8,128)(2,1)S(1)}, bf16[512,768]{1,0:T(8,128)(2,1)}, u32[]{:S(2)}, u32[]{:S(2)}) collective-permute-start(bf16[512,768]{1,0:T(8,128)(2,1)S(1)} %get-tuple-element.179.c0), channel_id=1, source_target_pairs={{0,8},{4,12},{8,0},{12,4},{1,9},{5,13},{9,1},{13,5},{2,10},{6,14},... | collective-permute-start | bytes 2359304 | tf_op jit(solution)/shard_map/ppermute | solution.py:635
  46.4 1.4 broadcast_select_fusion.8
  49.7 1.4 pad.20
  51.8 1.4 fusion.42
  53.2 13.0 %project.1 = (bf16[2048,768]{1,0:T(8,128)(2,1)}, bf16[2048,384]{1,0:T(8,128)(2,1)}, bf16[2048,384]{1,0:T(8,128)(2,1)}, bf16[2048,384]{1,0:T(8,128)(2,1)}, bf16[3...) custom-call(s32[8]{0:T(128)} %pad_add_fusion.info, ...), custom_call_target="tpu_custom_call" | custom-call | flops 37748736 | tf_op jit(solution)/shard_map/project/pallas_call | solution.py:150
  66.2 2.5 broadcast_select_fusion.3
  69.8 3.1 collective-permute-start.9
  72.9 11.0 %attend.2 = (bf16[1024,192]{1,0:T(8,128)(2,1)}, f32[192,1024]{1,0:T(8,128)}, f32[8,1024]{1,0:T(8,128)}) custom-call(bf16[2048,384]{1,0:T(8,128)(2,1)} %get-tuple-element.184.qa, bf16[2048,384]{1,0:T(8,128)(2,1)} %get-tuple-element.172.ka, bf16[384,2048]{1,0:T(8,128)(2,1)} %get-tuple-element.173.vt, f32[3,3,128,128]{3,2,1,0:T(8,128)} %get-tuple-element.174.near), custom_call_target="tpu_custom_call" | custom-call | flops 125829120 | tf_op jit(solution)/shard_map/attend/pallas_call | solution.py:236
  84.6 1.4 collective-permute-start.12
  86.7 11.3 %attend.3 = (bf16[1024,192]{1,0:T(8,128)(2,1)}, f32[192,1024]{1,0:T(8,128)}, f32[8,1024]{1,0:T(8,128)}) custom-call(bf16[2048,384]{1,0:T(8,128)(2,1)} %get-tuple-element.184.qa, bf16[2048,384]{1,0:T(8,128)(2,1)} %get-tuple-element.172.ka, bf16[384,2048]{1,0:T(8,128)(2,1)} %get-tuple-element.173.vt, f32[3,3,128,128]{3,2,1,0:T(8,128)} %get-tuple-element.174.near), custom_call_target="tpu_custom_call" | custom-call | flops 125829120 | tf_op jit(solution)/shard_map/attend/pallas_call | solution.py:236
  98.1 1.6 collective-permute-done.11.m2
  99.7 9.5 %collective-permute-done.12.m3 = bf16[1024,192]{1,0:T(8,128)(2,1)} collective-permute-done((bf16[1024,192]{1,0:T(8,128)(2,1)}, bf16[1024,192]{1,0:T(8,128)(2,1)}, u32[]{:S(2)}, u32[]{:S(2)}) %collective-permute-start.12) | collective-permute-done | bytes 393248 | tf_op jit(solution)/shard_map/ppermute | solution.py:635
  111.3 1.8 broadcast_select_fusion.1
  113.1 1.6 pad_maximum_fusion.w_ffn
  114.6 20.5 %middle.2 = (bf16[2,256,768]{2,1,0:T(8,128)(2,1)}, bf16[2,256,768]{2,1,0:T(8,128)(2,1)}, bf16[2,256,768]{2,1,0:T(8,128)(2,1)}, bf16[2,256,768]{2,1,0:T(8,128)(2,...) custom-call(s32[8]{0:T(128)} %pad_add_fusion.info, bf16[512,768]{1,0:T(8,128)(2,1)} %get-tuple-element.377.x0, ...), custom_call_target="tpu_custom_call" | custom-call | flops 188743680 | tf_op jit(solution)/shard_map/middle/pallas_call | solution.py:319
  136.2 1.9 collective-permute-done.19
  139.8 21.2 %middle.3 = (bf16[2,256,768]{2,1,0:T(8,128)(2,1)}, bf16[2,256,768]{2,1,0:T(8,128)(2,1)}, bf16[2,256,768]{2,1,0:T(8,128)(2,1)}, bf16[2,256,768]{2,1,0:T(8,128)(2,...) custom-call(s32[8]{0:T(128)} %pad_add_fusion.info, bf16[512,768]{1,0:T(8,128)(2,1)} %get-tuple-element.377.x0, ...), custom_call_target="tpu_custom_call" | custom-call | flops 188743680 | tf_op jit(solution)/shard_map/middle/pallas_call | solution.py:319
  162.0 2.4 collective-permute-done.22
  168.3 1.8 collective-permute-start.25
  174.6 29.8 %attend_back.2 = (bf16[1024,384]{1,0:T(8,128)(2,1)}, f32[2048,384]{1,0:T(8,128)}, f32[2048,384]{1,0:T(8,128)}, f32[3,3,128,128]{3,2,1,0:T(8,128)}, f32[192,768]{1,0:T(8,128)}, /*index=5*/f32[3,16,128]{2,1,0:T(8,128)}) custom-call(s32[8]{0:T(128)} %pad_add_fusion.info, bf16[2048,384]{1,0:T(8,128)(2,1)} %get-tuple-element.184.qa, ...), custom_call_target="tpu_custom_call" | custom-call | flops 251658240 | tf_op jit(solution)/shard_map/attend_back/pallas_call | solution.py:457
  205.1 1.8 collective-permute-start.28
  207.0 1.6 add_convert_fusion.2.sum_mine
  211.7 3.3 fusion.15
  215.9 30.1 %attend_back.3 = (bf16[1024,384]{1,0:T(8,128)(2,1)}, bf16[2048,384]{1,0:T(8,128)(2,1)}, bf16[2048,384]{1,0:T(8,128)(2,1)}, f32[3,3,128,128]{3,2,1,0:T(8,128)}, f...) custom-call(s32[8]{0:T(128)} %pad_add_fusion.info, bf16[2048,384]{1,0:T(8,128)(2,1)} %get-tuple-element.184.qa, ...), custom_call_target="tpu_custom_call" | custom-call | flops 251658240 | tf_op jit(solution)/shard_map/attend_back/pallas_call | solution.py:457
  246.0 1.4 broadcast_select_fusion.2
  247.4 9.6 %tail.1 = (bf16[4,256,768]{2,1,0:T(8,128)(2,1)}, bf16[4,256,768]{2,1,0:T(8,128)(2,1)}) custom-call(s32[8]{0:T(128)} %pad_add_fusion.info, bf16[1024,384]{1,0:T(8,128)(2,1)} %get-tuple-element.280.dq0, bf16[1024,384]{1,0:T(8,128)(2,1)} %get-tuple-element.281.dq1, bf16[2048,384]{1,0:T(8,128)(2,1)} %get-tuple-element.282.dk, ...), custom_call_target="tpu_custom_call" | custom-call | flops 56623104 | tf_op jit(solution)/shard_map/tail/pallas_call | solution.py:555
  258.8 1.3 select_convert_fusion
  263.2 3.2 bucket_sums.1
  266.4 1.4 select_reduce_fusion.1
  267.8 2.6 add_convert_fusion.1
  270.4 4.8 %collective-permute-start.31 = (bf16[2,256,768]{2,1,0:T(8,128)(2,1)}, bf16[2,256,768]{2,1,0:T(8,128)(2,1)}, u32[]{:S(2)}, u32[]{:S(2)}) collective-permute-start(bf16[2,256,768]{2,1,0:T(8,128)(2,1)} %add_convert_fusion.1), channel_id=1, source_target_pairs={{0,8},{4,12},{8,0},{12,4},{1,9},{5,13},{9,1},{13,5},{2,10},{6,14},... | collective-permute-start | bytes 2359304 | tf_op jit(solution)/shard_map/ppermute | solution.py:635
  280.0 8.6 %weights.1 = bf16[800,768]{1,0:T(8,128)(2,1)} custom-call(bf16[1024,384]{1,0:T(8,128)(2,1)} %get-tuple-element.280.dq0, bf16[1024,384]{1,0:T(8,128)(2,1)} %get-tuple-element.281.dq1, bf16[2048,384]{1,0:T(8,128)(2,1)} %get-tuple-element.282.dk, bf16[2048,384]{1,0:T(8,128)(2,1)} %get-tuple-element.283.dv, bf16[2048,768]{1,0:T(8,128)(2,1)} %get-tuple-element.170.normed, ...), custom_call_target="tpu_custom_call" | custom-call | flops 56623104 | tf_op jit(solution)/shard_map/weights/pallas_call | solution.py:605
  288.7 2.7 add_convert_fusion
  291.4 2.2 collective-permute-done.31
  293.6 2.2 multiply_reduce_fusion.2
  296.1 2.2 fusion.16
  298.4 1.6 fusion.9
  302.2 1.7 collective-permute-start.36
  303.9 1.9 collective-permute-done.36
  305.8 1.7 collective-permute-start.43
  308.9 1.3 collective-permute-start.32
  310.3 1.6 collective-permute-start.33
  311.9 11.8 %collective-permute-done.34 = bf16[800,384]{1,0:T(8,128)(2,1)} collective-permute-done((bf16[800,384]{1,0:T(8,128)(2,1)}, bf16[800,384]{1,0:T(8,128)(2,1)}, u32[]{:S(2)}, u32[]{:S(2)}) %collective-permute-start.34) | collective-permute-done | bytes 614432 | tf_op jit(solution)/shard_map/ppermute | solution.py:689
  323.6 2.0 add_convert_fusion.7
  325.7 12.7 %collective-permute-done.32 = bf16[512,768]{1,0:T(8,128)(2,1)S(1)} collective-permute-done((bf16[512,768]{1,0:T(8,128)(2,1)}, bf16[512,768]{1,0:T(8,128)(2,1)S(1)}, u32[]{:S(2)}, u32[]{:S(2)}) %collective-permute-start.32) | collective-permute-done | bytes 786464 | tf_op jit(solution)/shard_map/ppermute | solution.py:649
  339.3 2.0 convert_add_fusion
  341.4 1.8 collective-permute-start.41
  345.2 16.5 %collective-permute-start.40 = (bf16[800,384]{1,0:T(8,128)(2,1)S(1)}, bf16[800,384]{1,0:T(8,128)(2,1)S(1)}, u32[]{:S(2)}, u32[]{:S(2)}) collective-permute-start(bf16[800,384]{1,0:T(8,128)(2,1)S(1)} %broadcast_select_fusion.5), channel_id=1, source_target_pairs={{0,4},{4,0},{8,12},{12,8},{1,5},{5,1},{9,13},{13,9},{2,6},{6,2},{1... | collective-permute-start | bytes 1843208 | tf_op jit(solution)/shard_map/ppermute | solution.py:635
  362.3 1.4 copy-done.22
  364.0 1.6 pad_maximum_fusion.1
  365.6 8.9 %collective-permute-done.42 = f32[2,768]{1,0:T(2,128)S(1)} collective-permute-done((f32[2,768]{1,0:T(2,128)S(1)}, f32[2,768]{1,0:T(2,128)S(1)}, u32[]{:S(2)}, u32[]{:S(2)}) %collective-permute-start.42) | collective-permute-done | bytes 6176 | tf_op jit(solution)/shard_map/ppermute | solution.py:649
  375.2 1.6 slice_bitcast_fusion
  379.5 11.2 %collective-permute-done.46 = bf16[800,384]{1,0:T(8,128)(2,1)S(1)} collective-permute-done((bf16[800,384]{1,0:T(8,128)(2,1)S(1)}, bf16[800,384]{1,0:T(8,128)(2,1)S(1)}, u32[]{:S(2)}, u32[]{:S(2)}) %collective-permute-start.46) | collective-permute-done | bytes 614432 | tf_op jit(solution)/shard_map/ppermute | solution.py:635
  390.8 8.9 %collective-permute-done.45 = bf16[512,768]{1,0:T(8,128)(2,1)S(1)} collective-permute-done((bf16[512,768]{1,0:T(8,128)(2,1)S(1)}, bf16[512,768]{1,0:T(8,128)(2,1)S(1)}, u32[]{:S(2)}, u32[]{:S(2)}) %collective-permute-start.45) | collective-permute-done | bytes 786464 | tf_op jit(solution)/shard_map/ppermute | solution.py:649
  401.6 1.4 copy.35
  (273 shorter events, 56.0 us)
Async XLA Ops:
  7.2 197.9 %reduce-scatter.2.cloned.1.call-start = ((), (), s32[]{:S(2)}) async-start(), calls=%async_computation.1 | async-start | bytes 3538944 | tf_op jit(solution)/shard_map/reduce_scatter | solution.py:847
  7.3 10.9 %copy-start.34 = (bf16[768,384]{1,0:T(8,128)(2,1)S(1)}, bf16[768,384]{1,0:T(8,128)(2,1)}, u32[]{:S(2)}) copy-start(bf16[768,384]{1,0:T(8,128)(2,1)} %param.22) | copy-start | bytes 1769476
  10.4 8.9 %collective-permute-start.3 = (bf16[800,384]{1,0:T(8,128)(2,1)S(1)}, bf16[800,384]{1,0:T(8,128)(2,1)}, u32[]{:S(2)}, u32[]{:S(2)}) collective-permute-start(bf16[800,384]{1,0:T(8,128)(2,1)S(1)} %concatenate.37), channel_id=1, source_target_pairs={{4,6},{5,7},{6,4},{7,5},{8,9},{9,8},{10,11},{11,10},{12,15},{13,14... | collective-permute-start | bytes 1843208 | tf_op jit(solution)/shard_map/ppermute | solution.py:644
  11.9 22.8 %collective-permute-start.1 = (bf16[512,768]{1,0:T(8,128)(2,1)}, bf16[512,768]{1,0:T(8,128)(2,1)}, u32[]{:S(2)}, u32[]{:S(2)}) collective-permute-start(bf16[512,768]{1,0:T(8,128)(2,1)} %get-tuple-element.377.x0), channel_id=1, source_target_pairs={{0,8},{4,12},{8,0},{12,4},{1,9},{5,13},{9,1},{13,5},{2,10},{6,14},... | collective-permute-start | bytes 2359304 | tf_op jit(solution)/shard_map/ppermute | solution.py:635
  16.9 36.3 %collective-permute-start = (bf16[512,768]{1,0:T(8,128)(2,1)}, bf16[512,768]{1,0:T(8,128)(2,1)}, u32[]{:S(2)}, u32[]{:S(2)}) collective-permute-start(bf16[512,768]{1,0:T(8,128)(2,1)} %get-tuple-element.377.x0), channel_id=1, source_target_pairs={{0,4},{4,0},{8,12},{12,8},{1,5},{5,1},{9,13},{13,9},{2,6},{6,2},{1... | collective-permute-start | bytes 2359304 | tf_op jit(solution)/shard_map/ppermute | solution.py:635
  19.3 8.9 %copy-start.18 = (bf16[800,384]{1,0:T(8,128)(2,1)}, bf16[800,384]{1,0:T(8,128)(2,1)S(1)}, u32[]{:S(2)}) copy-start(bf16[800,384]{1,0:T(8,128)(2,1)S(1)} %broadcast_select_fusion.6) | copy-start | bytes 1843204
  19.4 27.0 %collective-permute-start.4 = (bf16[800,384]{1,0:T(8,128)(2,1)S(1)}, bf16[800,384]{1,0:T(8,128)(2,1)}, u32[]{:S(2)}, u32[]{:S(2)}) collective-permute-start(bf16[800,384]{1,0:T(8,128)(2,1)S(1)} %broadcast_select_fusion.6), channel_id=1, source_target_pairs={{0,16},{16,0},{1,17},{17,1},{2,18},{18,2},{3,19},{19,3},{4,20},{20... | collective-permute-start | bytes 1843208 | tf_op jit(solution)/shard_map/ppermute | solution.py:689
  23.7 42.5 %collective-permute-start.6 = (bf16[384,1536]{1,0:T(8,128)(2,1)}, bf16[384,1536]{1,0:T(8,128)(2,1)}, u32[]{:S(2)}, u32[]{:S(2)}) collective-permute-start(bf16[384,1536]{1,0:T(8,128)(2,1)} %pad_maximum_fusion.2), channel_id=1, source_target_pairs={{4,6},{5,7},{6,4},{7,5},{8,9},{9,8},{10,11},{11,10},{12,15},{13,14... | collective-permute-start | bytes 3538952 | tf_op jit(solution)/shard_map/ppermute | solution.py:644
  28.2 20.4 %copy-start = (bf16[512,768]{1,0:T(8,128)(2,1)}, bf16[512,768]{1,0:T(8,128)(2,1)S(1)}, u32[]{:S(2)}) copy-start(bf16[512,768]{1,0:T(8,128)(2,1)S(1)} %get-tuple-element.179.c0) | copy-start | bytes 2359300
  34.7 18.5 %collective-permute-start.2 = (bf16[512,768]{1,0:T(8,128)(2,1)}, bf16[512,768]{1,0:T(8,128)(2,1)}, u32[]{:S(2)}, u32[]{:S(2)}) collective-permute-start(bf16[512,768]{1,0:T(8,128)(2,1)} %collective-permute-done.1.x2), channel_id=1, source_target_pairs={{0,4},{4,0},{8,12},{12,8},{1,5},{5,1},{9,13},{13,9},{2,6},{6,2},{1... | collective-permute-start | bytes 2359304 | tf_op jit(solution)/shard_map/ppermute | solution.py:635
  41.5 27.2 %collective-permute-start.5 = (bf16[512,768]{1,0:T(8,128)(2,1)S(1)}, bf16[512,768]{1,0:T(8,128)(2,1)}, u32[]{:S(2)}, u32[]{:S(2)}) collective-permute-start(bf16[512,768]{1,0:T(8,128)(2,1)S(1)} %get-tuple-element.179.c0), channel_id=1, source_target_pairs={{0,8},{4,12},{8,0},{12,4},{1,9},{5,13},{9,1},{13,5},{2,10},{6,14},... | collective-permute-start | bytes 2359304 | tf_op jit(solution)/shard_map/ppermute | solution.py:635
  46.4 37.6 %collective-permute-start.7 = (bf16[512,768]{1,0:T(8,128)(2,1)S(1)}, bf16[512,768]{1,0:T(8,128)(2,1)}, u32[]{:S(2)}, u32[]{:S(2)}) collective-permute-start(bf16[512,768]{1,0:T(8,128)(2,1)S(1)} %get-tuple-element.179.c0), channel_id=1, source_target_pairs={{0,4},{4,0},{8,12},{12,8},{1,5},{5,1},{9,13},{13,9},{2,6},{6,2},{1... | collective-permute-start | bytes 2359304 | tf_op jit(solution)/shard_map/ppermute | solution.py:635
  68.7 15.3 %collective-permute-start.8 = (bf16[512,768]{1,0:T(8,128)(2,1)}, bf16[512,768]{1,0:T(8,128)(2,1)}, u32[]{:S(2)}, u32[]{:S(2)}) collective-permute-start(bf16[512,768]{1,0:T(8,128)(2,1)} %collective-permute-done.5.c2), channel_id=1, source_target_pairs={{0,4},{4,0},{8,12},{12,8},{1,5},{5,1},{9,13},{13,9},{2,6},{6,2},{1... | collective-permute-start | bytes 2359304 | tf_op jit(solution)/shard_map/ppermute | solution.py:635
  69.2 39.9 %collective-permute-start.15 = (bf16[384,1536]{1,0:T(8,128)(2,1)}, bf16[384,1536]{1,0:T(8,128)(2,1)}, u32[]{:S(2)}, u32[]{:S(2)}) collective-permute-start(bf16[384,1536]{1,0:T(8,128)(2,1)} %broadcast_select_fusion.3), channel_id=1, source_target_pairs={{0,16},{16,0},{1,17},{17,1},{2,18},{18,2},{3,19},{19,3},{4,20},{20... | collective-permute-start | bytes 3538952 | tf_op jit(solution)/shard_map/ppermute | solution.py:689
  69.8 14.2 %copy-start.13 = (bf16[192,768]{1,0:T(8,128)(2,1)}, bf16[192,768]{1,0:T(8,128)(2,1)S(1)}, u32[]{:S(2)}) copy-start(bf16[192,768]{1,0:T(8,128)(2,1)S(1)} %fusion.29.w0) | copy-start | bytes 884740
  69.8 14.2 %collective-permute-start.9 = (bf16[192,768]{1,0:T(8,128)(2,1)S(1)}, bf16[192,768]{1,0:T(8,128)(2,1)S(1)}, u32[]{:S(2)}, u32[]{:S(2)}) collective-permute-start(bf16[192,768]{1,0:T(8,128)(2,1)S(1)} %fusion.29.w0), channel_id=1, source_target_pairs={{0,8},{4,12},{8,0},{12,4},{1,9},{5,13},{9,1},{13,5},{2,10},{6,14},... | collective-permute-start | bytes 884744 | tf_op jit(solution)/shard_map/ppermute | solution.py:635
  72.9 13.1 %collective-permute-start.13 = (bf16[192,768]{1,0:T(8,128)(2,1)S(1)}, bf16[192,768]{1,0:T(8,128)(2,1)S(1)}, u32[]{:S(2)}, u32[]{:S(2)}) collective-permute-start(bf16[192,768]{1,0:T(8,128)(2,1)S(1)} %fusion.29.w0), channel_id=1, source_target_pairs={{0,4},{4,0},{8,12},{12,8},{1,5},{5,1},{9,13},{13,9},{2,6},{6,2},{1... | collective-permute-start | bytes 884744 | tf_op jit(solution)/shard_map/ppermute | solution.py:635
  84.0 14.1 %copy-start.23 = (bf16[192,768]{1,0:T(8,128)(2,1)}, bf16[192,768]{1,0:T(8,128)(2,1)S(1)}, u32[]{:S(2)}) copy-start(bf16[192,768]{1,0:T(8,128)(2,1)S(1)} %collective-permute-done.9.w2) | copy-start | bytes 884740
  84.0 14.1 %collective-permute-start.10 = (bf16[1024,192]{1,0:T(8,128)(2,1)}, bf16[1024,192]{1,0:T(8,128)(2,1)S(1)}, u32[]{:S(2)}, u32[]{:S(2)}) collective-permute-start(bf16[1024,192]{1,0:T(8,128)(2,1)} %get-tuple-element.190.m0), channel_id=1, source_target_pairs={{0,4},{4,0},{8,12},{12,8},{1,5},{5,1},{9,13},{13,9},{2,6},{6,2},{1... | collective-permute-start | bytes 1179656 | tf_op jit(solution)/shard_map/ppermute | solution.py:635
  84.6 15.1 %collective-permute-start.11 = (bf16[1024,192]{1,0:T(8,128)(2,1)}, bf16[1024,192]{1,0:T(8,128)(2,1)}, u32[]{:S(2)}, u32[]{:S(2)}) collective-permute-start(bf16[1024,192]{1,0:T(8,128)(2,1)} %get-tuple-element.190.m0), channel_id=1, source_target_pairs={{0,8},{4,12},{8,0},{12,4},{1,9},{5,13},{9,1},{13,5},{2,10},{6,14},... | collective-permute-start | bytes 1179656 | tf_op jit(solution)/shard_map/ppermute | solution.py:635
  84.6 24.5 %collective-permute-start.12 = (bf16[1024,192]{1,0:T(8,128)(2,1)}, bf16[1024,192]{1,0:T(8,128)(2,1)}, u32[]{:S(2)}, u32[]{:S(2)}) collective-permute-start(bf16[1024,192]{1,0:T(8,128)(2,1)} %get-tuple-element.190.m0), channel_id=1, source_target_pairs={{0,12},{4,8},{8,4},{12,0},{1,13},{5,9},{9,5},{13,1},{2,14},{6,10},... | collective-permute-start | bytes 1179656 | tf_op jit(solution)/shard_map/ppermute | solution.py:635
  86.0 12.0 %copy-start.24 = (bf16[192,768]{1,0:T(8,128)(2,1)}, bf16[192,768]{1,0:T(8,128)(2,1)S(1)}, u32[]{:S(2)}) copy-start(bf16[192,768]{1,0:T(8,128)(2,1)S(1)} %collective-permute-done.13.w1) | copy-start | bytes 884740
  86.0 12.0 %collective-permute-start.14 = (bf16[192,768]{1,0:T(8,128)(2,1)S(1)}, bf16[192,768]{1,0:T(8,128)(2,1)S(1)}, u32[]{:S(2)}, u32[]{:S(2)}) collective-permute-start(bf16[192,768]{1,0:T(8,128)(2,1)S(1)} %collective-permute-done.9.w2), channel_id=1, source_target_pairs={{0,4},{4,0},{8,12},{12,8},{1,5},{5,1},{9,13},{13,9},{2,6},{6,2},{1... | collective-permute-start | bytes 884744 | tf_op jit(solution)/shard_map/ppermute | solution.py:635
  98.0 15.0 %copy-start.25 = (bf16[192,768]{1,0:T(8,128)(2,1)}, bf16[192,768]{1,0:T(8,128)(2,1)S(1)}, u32[]{:S(2)}) copy-start(bf16[192,768]{1,0:T(8,128)(2,1)S(1)} %collective-permute-done.14.w3) | copy-start | bytes 884740
  98.1 11.1 %copy-start.38 = (bf16[1024,192]{1,0:T(8,128)(2,1)}, bf16[1024,192]{1,0:T(8,128)(2,1)S(1)}, u32[]{:S(2)}) copy-start(bf16[1024,192]{1,0:T(8,128)(2,1)S(1)} %collective-permute-done.10.m1) | copy-start | bytes 1179652
  109.2 26.0 %collective-permute-start.16 = (bf16[1024,192]{1,0:T(8,128)(2,1)}, bf16[1024,192]{1,0:T(8,128)(2,1)S(1)}, u32[]{:S(2)}, u32[]{:S(2)}) collective-permute-start(bf16[1024,192]{1,0:T(8,128)(2,1)} %get-tuple-element.214.m0), channel_id=1, source_target_pairs={{0,4},{4,0},{8,12},{12,8},{1,5},{5,1},{9,13},{13,9},{2,6},{6,2},{1... | collective-permute-start | bytes 1179656 | tf_op jit(solution)/shard_map/ppermute | solution.py:635
  109.9 25.3 %collective-permute-start.17 = (bf16[1024,192]{1,0:T(8,128)(2,1)}, bf16[1024,192]{1,0:T(8,128)(2,1)S(1)}, u32[]{:S(2)}, u32[]{:S(2)}) collective-permute-start(bf16[1024,192]{1,0:T(8,128)(2,1)} %get-tuple-element.214.m0), channel_id=1, source_target_pairs={{0,8},{4,12},{8,0},{12,4},{1,9},{5,13},{9,1},{13,5},{2,10},{6,14},... | collective-permute-start | bytes 1179656 | tf_op jit(solution)/shard_map/ppermute | solution.py:635
  110.1 25.0 %collective-permute-start.18 = (bf16[1024,192]{1,0:T(8,128)(2,1)}, bf16[1024,192]{1,0:T(8,128)(2,1)S(1)}, u32[]{:S(2)}, u32[]{:S(2)}) collective-permute-start(bf16[1024,192]{1,0:T(8,128)(2,1)} %get-tuple-element.214.m0), channel_id=1, source_target_pairs={{0,12},{4,8},{8,4},{12,0},{1,13},{5,9},{9,5},{13,1},{2,14},{6,10},... | collective-permute-start | bytes 1179656 | tf_op jit(solution)/shard_map/ppermute | solution.py:635
  135.2 2.9 collective-permute-start.19
  139.4 21.6 %collective-permute-start.20 = (bf16[2,256,768]{2,1,0:T(8,128)(2,1)S(1)}, bf16[2,256,768]{2,1,0:T(8,128)(2,1)S(1)}, u32[]{:S(2)}, u32[]{:S(2)}) collective-permute-start(bf16[2,256,768]{2,1,0:T(8,128)(2,1)S(1)} %add_convert_fusion.5), channel_id=1, source_target_pairs={{0,8},{4,12},{8,0},{12,4},{1,9},{5,13},{9,1},{13,5},{2,10},{6,14},... | collective-permute-start | bytes 2359304 | tf_op jit(solution)/shard_map/ppermute | solution.py:635
  161.9 2.5 collective-permute-start.22
  165.7 172.7 %all-gather.3.cloned.1.call-start = ((), (), s32[]{:S(2)}) async-start(), calls=%async_computation.2 | async-start | bytes 3932160 | tf_op jit(solution)/shard_map/all_gather | solution.py:872
  166.2 3.9 collective-permute-start.23
  166.4 4.0 collective-permute-start.24
  168.1 5.6 %collective-permute-start.21 = (bf16[2,256,768]{2,1,0:T(8,128)(2,1)S(1)}, bf16[2,256,768]{2,1,0:T(8,128)(2,1)S(1)}, u32[]{:S(2)}, u32[]{:S(2)}) collective-permute-start(bf16[2,256,768]{2,1,0:T(8,128)(2,1)S(1)} %add_convert_fusion.4.sum_mine), channel_id=1, source_target_pairs={{0,4},{4,0},{8,12},{12,8},{1,5},{5,1},{9,13},{13,9},{2,6},{6,2},{1... | collective-permute-start | bytes 2359304 | tf_op jit(solution)/shard_map/ppermute | solution.py:635
  168.3 36.1 %collective-permute-start.25 = (bf16[2,256,768]{2,1,0:T(8,128)(2,1)S(1)}, bf16[2,256,768]{2,1,0:T(8,128)(2,1)}, u32[]{:S(2)}, u32[]{:S(2)}) collective-permute-start(bf16[2,256,768]{2,1,0:T(8,128)(2,1)S(1)} %add_convert_fusion.3), channel_id=1, source_target_pairs={{0,8},{4,12},{8,0},{12,4},{1,9},{5,13},{9,1},{13,5},{2,10},{6,14},... | collective-permute-start | bytes 2359304 | tf_op jit(solution)/shard_map/ppermute | solution.py:635
  172.4 32.7 %collective-permute-start.26 = (bf16[2,256,768]{2,1,0:T(8,128)(2,1)}, bf16[2,256,768]{2,1,0:T(8,128)(2,1)}, u32[]{:S(2)}, u32[]{:S(2)}) collective-permute-start(bf16[2,256,768]{2,1,0:T(8,128)(2,1)} %pad_maximum_fusion.3), channel_id=1, source_target_pairs={{0,8},{4,12},{8,0},{12,4},{1,9},{5,13},{9,1},{13,5},{2,10},{6,14},... | collective-permute-start | bytes 2359304 | tf_op jit(solution)/shard_map/ppermute | solution.py:635
  205.1 40.9 %collective-permute-start.28 = (bf16[384,1536]{1,0:T(8,128)(2,1)}, bf16[384,1536]{1,0:T(8,128)(2,1)}, u32[]{:S(2)}, u32[]{:S(2)}) collective-permute-start(bf16[384,1536]{1,0:T(8,128)(2,1)} %reduce-scatter.2.cloned.1.call-done), channel_id=1, source_target_pairs={{4,6},{6,4},{7,5},{8,9},{10,11},{11,10},{12,15},{14,13},{15,12},{2... | collective-permute-start | bytes 3538952 | tf_op jit(solution)/shard_map/ppermute | solution.py:644
  208.5 7.4 %collective-permute-start.27 = (bf16[2,256,768]{2,1,0:T(8,128)(2,1)S(1)}, bf16[2,256,768]{2,1,0:T(8,128)(2,1)}, u32[]{:S(2)}, u32[]{:S(2)}) collective-permute-start(bf16[2,256,768]{2,1,0:T(8,128)(2,1)S(1)} %add_convert_fusion.2.sum_mine), channel_id=1, source_target_pairs={{0,4},{4,0},{8,12},{12,8},{1,5},{5,1},{9,13},{13,9},{2,6},{6,2},{1... | collective-permute-start | bytes 2359304 | tf_op jit(solution)/shard_map/ppermute | solution.py:635
  257.1 10.7 %collective-permute-start.29 = (bf16[4,256,768]{2,1,0:T(8,128)(2,1)}, bf16[4,256,768]{2,1,0:T(8,128)(2,1)}, u32[]{:S(2)}, u32[]{:S(2)}) collective-permute-start(bf16[4,256,768]{2,1,0:T(8,128)(2,1)} %get-tuple-element.274), channel_id=1, source_target_pairs={{0,4},{4,0},{8,12},{12,8},{1,5},{5,1},{9,13},{13,9},{2,6},{6,2},{1... | collective-permute-start | bytes 4718600 | tf_op jit(solution)/shard_map/ppermute | solution.py:635
  257.8 10.0 %collective-permute-start.30 = (bf16[384,1536]{1,0:T(8,128)(2,1)S(1)}, bf16[384,1536]{1,0:T(8,128)(2,1)}, u32[]{:S(2)}, u32[]{:S(2)}) collective-permute-start(bf16[384,1536]{1,0:T(8,128)(2,1)S(1)} %broadcast_select_fusion.2), channel_id=1, source_target_pairs={{0,4},{4,0},{8,12},{12,8},{1,5},{5,1},{9,13},{13,9},{2,6},{6,2},{1... | collective-permute-start | bytes 3538952 | tf_op jit(solution)/shard_map/ppermute | solution.py:635
  267.8 8.3 %copy-start.51 = (f32[3]{0:T(128)S(1)}, f32[3]{0:T(128)}, u32[]{:S(2)}) copy-start(f32[3]{0:T(128)} %get-tuple-element.358) | copy-start | bytes 40
  270.4 23.1 %collective-permute-start.31 = (bf16[2,256,768]{2,1,0:T(8,128)(2,1)}, bf16[2,256,768]{2,1,0:T(8,128)(2,1)}, u32[]{:S(2)}, u32[]{:S(2)}) collective-permute-start(bf16[2,256,768]{2,1,0:T(8,128)(2,1)} %add_convert_fusion.1), channel_id=1, source_target_pairs={{0,8},{4,12},{8,0},{12,4},{1,9},{5,13},{9,1},{13,5},{2,10},{6,14},... | collective-permute-start | bytes 2359304 | tf_op jit(solution)/shard_map/ppermute | solution.py:635
  288.6 7.2 %copy-start.8 = (f32[2,256,768]{2,1,0:T(8,128)S(1)}, f32[2,256,768]{2,1,0:T(8,128)}, u32[]{:S(2)}) copy-start(f32[2,256,768]{2,1,0:T(8,128)} %select_convert_fusion) | copy-start | bytes 4718596
  300.0 7.5 %copy-start.9 = (bf16[800,768]{1,0:T(8,128)(2,1)S(1)}, bf16[800,768]{1,0:T(8,128)(2,1)}, u32[]{:S(2)}) copy-start(bf16[800,768]{1,0:T(8,128)(2,1)} %weights.1) | copy-start | bytes 3686404
  301.0 1.2 collective-permute-start.35
  302.2 3.6 collective-permute-start.36
  305.8 33.5 %collective-permute-start.43 = (bf16[384,1536]{1,0:T(8,128)(2,1)}, bf16[384,1536]{1,0:T(8,128)(2,1)}, u32[]{:S(2)}, u32[]{:S(2)}) collective-permute-start(bf16[384,1536]{1,0:T(8,128)(2,1)} %add_convert_fusion), channel_id=1, source_target_pairs={{0,8},{4,12},{8,0},{12,4},{1,9},{5,13},{9,1},{13,5},{2,10},{6,14},... | collective-permute-start | bytes 3538952 | tf_op jit(solution)/shard_map/ppermute | solution.py:635
  308.4 15.2 %collective-permute-start.34 = (bf16[800,384]{1,0:T(8,128)(2,1)}, bf16[800,384]{1,0:T(8,128)(2,1)}, u32[]{:S(2)}, u32[]{:S(2)}) collective-permute-start(bf16[800,384]{1,0:T(8,128)(2,1)} %constant_dynamic-slice_fusion.1), channel_id=1, source_target_pairs={{0,16},{16,0},{1,17},{17,1},{2,18},{18,2},{3,19},{19,3},{4,20},{20... | collective-permute-start | bytes 1843208 | tf_op jit(solution)/shard_map/ppermute | solution.py:689
  308.9 29.4 %collective-permute-start.32 = (bf16[512,768]{1,0:T(8,128)(2,1)}, bf16[512,768]{1,0:T(8,128)(2,1)S(1)}, u32[]{:S(2)}, u32[]{:S(2)}) collective-permute-start(bf16[512,768]{1,0:T(8,128)(2,1)} %pad_maximum_fusion.5), channel_id=1, source_target_pairs={{0,1},{2,3},{4,5},{6,7},{8,9},{10,11},{12,13},{14,15},{16,17},{18,... | collective-permute-start | bytes 2359304 | tf_op jit(solution)/shard_map/ppermute | solution.py:649
  310.3 28.1 %collective-permute-start.33 = (bf16[512,768]{1,0:T(8,128)(2,1)}, bf16[512,768]{1,0:T(8,128)(2,1)}, u32[]{:S(2)}, u32[]{:S(2)}) collective-permute-start(bf16[512,768]{1,0:T(8,128)(2,1)} %pad_maximum_fusion.5), channel_id=1, source_target_pairs={{3,2},{2,1},{7,6},{6,5},{11,10},{10,9},{15,14},{14,13},{19,18},{18... | collective-permute-start | bytes 2359304 | tf_op jit(solution)/shard_map/ppermute | solution.py:649
  338.4 6.8 %collective-permute-start.39 = (bf16[800,384]{1,0:T(8,128)(2,1)}, bf16[800,384]{1,0:T(8,128)(2,1)S(1)}, u32[]{:S(2)}, u32[]{:S(2)}) collective-permute-start(bf16[800,384]{1,0:T(8,128)(2,1)} %add_convert_fusion.7), channel_id=1, source_target_pairs={{4,6},{6,4},{7,5},{8,9},{10,11},{11,10},{12,15},{14,13},{15,12},{2... | collective-permute-start | bytes 1843208 | tf_op jit(solution)/shard_map/ppermute | solution.py:644
  341.4 22.5 %collective-permute-start.41 = (f32[2,768]{1,0:T(2,128)S(1)}, f32[2,768]{1,0:T(2,128)S(1)}, u32[]{:S(2)}, u32[]{:S(2)}) collective-permute-start(f32[2,768]{1,0:T(2,128)S(1)} %add.384), channel_id=1, source_target_pairs={{0,16},{16,0},{1,17},{17,1},{2,18},{18,2},{3,19},{19,3},{4,20},{20... | collective-permute-start | bytes 18440 | tf_op jit(solution)/shard_map/ppermute | solution.py:689
  343.1 31.5 %collective-permute-start.37 = (bf16[512,768]{1,0:T(8,128)(2,1)S(1)}, bf16[512,768]{1,0:T(8,128)(2,1)S(1)}, u32[]{:S(2)}, u32[]{:S(2)}) collective-permute-start(bf16[512,768]{1,0:T(8,128)(2,1)S(1)} %collective-permute-done.32), channel_id=1, source_target_pairs={{1,2},{5,6},{9,10},{13,14},{17,18},{21,22},{25,26},{29,30}} | collective-permute-start | bytes 2359304 | tf_op jit(solution)/shard_map/ppermute | solution.py:649
  343.8 30.8 %collective-permute-start.38 = (bf16[512,768]{1,0:T(8,128)(2,1)}, bf16[512,768]{1,0:T(8,128)(2,1)S(1)}, u32[]{:S(2)}, u32[]{:S(2)}) collective-permute-start(bf16[512,768]{1,0:T(8,128)(2,1)} %collective-permute-done.33), channel_id=1, source_target_pairs={{2,1},{1,0},{6,5},{5,4},{10,9},{9,8},{14,13},{13,12},{18,17},{17,1... | collective-permute-start | bytes 2359304 | tf_op jit(solution)/shard_map/ppermute | solution.py:649
  345.2 29.2 %collective-permute-start.40 = (bf16[800,384]{1,0:T(8,128)(2,1)S(1)}, bf16[800,384]{1,0:T(8,128)(2,1)S(1)}, u32[]{:S(2)}, u32[]{:S(2)}) collective-permute-start(bf16[800,384]{1,0:T(8,128)(2,1)S(1)} %broadcast_select_fusion.5), channel_id=1, source_target_pairs={{0,4},{4,0},{8,12},{12,8},{1,5},{5,1},{9,13},{13,9},{2,6},{6,2},{1... | collective-permute-start | bytes 1843208 | tf_op jit(solution)/shard_map/ppermute | solution.py:635
  363.9 10.6 %collective-permute-start.42 = (f32[2,768]{1,0:T(2,128)S(1)}, f32[2,768]{1,0:T(2,128)S(1)}, u32[]{:S(2)}, u32[]{:S(2)}) collective-permute-start(f32[2,768]{1,0:T(2,128)S(1)} %add.386), channel_id=1, source_target_pairs={{0,1},{1,0},{2,3},{3,2},{4,5},{5,4},{6,7},{7,6},{8,9},{9,8},{10,11... | collective-permute-start | bytes 18440 | tf_op jit(solution)/shard_map/ppermute | solution.py:649
  374.7 4.8 %collective-permute-start.47 = (f32[2,768]{1,0:T(2,128)S(1)}, f32[2,768]{1,0:T(2,128)S(1)}, u32[]{:S(2)}, u32[]{:S(2)}) collective-permute-start(f32[2,768]{1,0:T(2,128)S(1)} %add.387), channel_id=1, source_target_pairs={{0,2},{1,3},{2,0},{3,1},{4,6},{5,7},{6,4},{7,5},{8,10},{9,11},{10,... | collective-permute-start | bytes 18440 | tf_op jit(solution)/shard_map/ppermute | solution.py:649
  374.7 15.9 %collective-permute-start.46 = (bf16[800,384]{1,0:T(8,128)(2,1)S(1)}, bf16[800,384]{1,0:T(8,128)(2,1)S(1)}, u32[]{:S(2)}, u32[]{:S(2)}) collective-permute-start(bf16[800,384]{1,0:T(8,128)(2,1)S(1)} %add_convert_fusion.6), channel_id=1, source_target_pairs={{0,8},{4,12},{8,0},{12,4},{1,9},{5,13},{9,1},{13,5},{2,10},{6,14},... | collective-permute-start | bytes 1843208 | tf_op jit(solution)/shard_map/ppermute | solution.py:635
  376.8 14.0 %collective-permute-start.44 = (bf16[512,768]{1,0:T(8,128)(2,1)S(1)}, bf16[512,768]{1,0:T(8,128)(2,1)S(1)}, u32[]{:S(2)}, u32[]{:S(2)}) collective-permute-start(bf16[512,768]{1,0:T(8,128)(2,1)S(1)} %collective-permute-done.37), channel_id=1, source_target_pairs={{2,3},{6,7},{10,11},{14,15},{18,19},{22,23},{26,27},{30,31}} | collective-permute-start | bytes 2359304 | tf_op jit(solution)/shard_map/ppermute | solution.py:649
  377.5 22.2 %collective-permute-start.45 = (bf16[512,768]{1,0:T(8,128)(2,1)S(1)}, bf16[512,768]{1,0:T(8,128)(2,1)S(1)}, u32[]{:S(2)}, u32[]{:S(2)}) collective-permute-start(bf16[512,768]{1,0:T(8,128)(2,1)S(1)} %collective-permute-done.38), channel_id=1, source_target_pairs={{1,0},{5,4},{9,8},{13,12},{17,16},{21,20},{25,24},{29,28}} | collective-permute-start | bytes 2359304 | tf_op jit(solution)/shard_map/ppermute | solution.py:649
  379.4 22.2 %copy-start.20 = (bf16[3,512,768]{2,1,0:T(8,128)(2,1)}, bf16[3,512,768]{2,1,0:T(8,128)(2,1)S(1)}, u32[]{:S(2)}) copy-start(bf16[3,512,768]{2,1,0:T(8,128)(2,1)S(1)} %bitcast_dynamic-update-slice_fusion.2) | copy-start | bytes 7077892
  390.8 10.9 %copy-start.12 = (f32[768,384]{0,1:T(8,128)S(1)}, f32[768,384]{0,1:T(8,128)}, u32[]{:S(2)}) copy-start(f32[768,384]{0,1:T(8,128)} %get-tuple-element.347) | copy-start | bytes 3538948
  390.8 9.8 %copy-start.31 = (bf16[512,768]{1,0:T(8,128)(2,1)}, bf16[512,768]{1,0:T(8,128)(2,1)S(1)}, u32[]{:S(2)}) copy-start(bf16[512,768]{1,0:T(8,128)(2,1)S(1)} %collective-permute-done.44) | copy-start | bytes 2359300
  (44 other events, 116.8 us)
Sparse Core Ops, SparseCore 0:
  165.8 35.6 reduce-scatter.1
  260.3 72.4 all-gather.2
where the time goes:
time: 419 us; the launch traced here: 414 us
  Pallas kernels  158 us (38%)
  waiting for transfers between devices  81.3 us (19%)
  starting transfers between devices  73.3 us (17%)
  other arithmetic  64.3 us (15%)
  local copies, waits for them, and re-layouts  21.1 us (5%)
  between operations  15.4 us (4%)
    pallas_call x2, Pallas kernels, attend_back(): pl.pallas_call(functools.partial(backward_kernel, per, offset, kc), grid_...  59.9 us
    ppermute x32, starting transfers between devices, swap_seq(): return lax.ppermute(value, 'seq', [(i, i ^ bit) for i in range(RANKS)])  55.6 us
    pallas_call x2, Pallas kernels, middle(): pl.pallas_call(functools.partial(middle_kernel, given is None), grid_spec...  41.7 us
    ppermute x32, waiting for transfers between devices, swap_seq(): return lax.ppermute(value, 'seq', [(i, i ^ bit) for i in range(RANKS)])  39 us
    ppermute x8, waiting for transfers between devices, along_tensor(): return lax.ppermute(value, 'tensor', pairs)  30.5 us
    pallas_call x2, Pallas kernels, attend(): pl.pallas_call(functools.partial(forward_kernel, heads, per, offset), gri...  22.3 us
    pallas_call x1, Pallas kernels, project(): pl.pallas_call(functools.partial(project_kernel, heads, per), grid_spec=p...  13 us
    ppermute x4, waiting for transfers between devices, swap_dp(): return lax.ppermute(value, 'dp', [(0, 1), (1, 0)])  11.8 us
  transfers between devices with their start and end apart: 50, of which 14 were waited for; matrix products, arithmetic and copies ran while one was open for 16% of the time, Pallas kernels for 36%

commit v1 on v0

--- a/solution.py
+++ b/solution.py
@@ -374,13 +374,18 @@
 
     @pl.when(head == 0)
     def _():
-        even = info[2 * step] % 2 == 0
-        mine, other = sum_mine[0], sum_other[0]
-        d_norm = jnp.concatenate(
-            [jnp.where(even, mine, other), jnp.where(even, other, mine)], axis=0
-        ).astype(FULL)
+        even = info[0] % 2 == 0
+        blocks = []
+        for k in range(sum_mine.shape[0]):
+            mine, other = sum_mine[k], sum_other[k]
+            blocks += [jnp.where(even, mine, other), jnp.where(even, other, mine)]
+        d_norm = jnp.concatenate(blocks, axis=0).astype(FULL)
         cot = jnp.concatenate(
-            [pick_block(info[2 * step + k], (c0, c1, c2, c3)) for k in range(2)], axis=0
+            [
+                pick_block(info[len(blocks) * step + k], (c0, c1, c2, c3))
+                for k in range(len(blocks))
+            ],
+            axis=0,
         ).astype(FULL)
         resid = resid_ref[...]
         scale = lax.rsqrt(jnp.mean(resid * resid, axis=-1, keepdims=True) + EPSILON)
@@ -443,7 +448,7 @@
     heads = wide // TILE
     model = resid.shape[1]
     rows = total // SPLIT // RANKS
-    bq = 2 * rows
+    bq = RANKS * rows
     span = total // SPLIT
     steps = span // bq
     offset = part * steps
@@ -465,7 +470,7 @@
                 pl.BlockSpec((TILE, total), lambda h, i, c: (h, 0)),
                 head_cols,
             ]
-            + [pl.BlockSpec((1, rows, model), lambda h, i, c: (once(h, i), 0, 0))] * 2
+            + [pl.BlockSpec((2, rows, model), lambda h, i, c: (once(h, i), 0, 0))] * 2
             + [pl.BlockSpec((bq, model), lambda h, i, c: (once(h, i), 0))]
             + [pl.BlockSpec((rows, model), lambda h, i, c: (part, 0))] * RANKS
             + [

time: 419 us -> 417 us (level)
    pallas_call x2, Pallas kernels: 59.9 us -> 55.4 us  [attend_back(): pl.pallas_call(functools.partial(backward_kernel, per, offset, kc), grid_...]
  transfers between devices with their start and end apart: 50 -> 50, of which waited for: 14 -> 14; matrix products, arithmetic and copies ran while one was open for 16% -> 16% of each run, Pallas kernels for 36% -> 35%
where the time goes in v1:
time: 417 us; the launch traced here: 412 us
  Pallas kernels  154 us (37%)
  waiting for transfers between devices  83.3 us (20%)
  starting transfers between devices  73.2 us (18%)
  other arithmetic  64.3 us (15%)
  local copies, waits for them, and re-layouts  21.1 us (5%)
  between operations  15.6 us (4%)
    ppermute x32, starting transfers between devices, swap_seq(): return lax.ppermute(value, 'seq', [(i, i ^ bit) for i in range(RANKS)])  55.6 us
    pallas_call x2, Pallas kernels, attend_back(): pl.pallas_call(functools.partial(backward_kernel, per, offset, kc), grid_...  55.4 us
    pallas_call x2, Pallas kernels, middle(): pl.pallas_call(functools.partial(middle_kernel, given is None), grid_spec...  41.7 us
    ppermute x32, waiting for transfers between devices, swap_seq(): return lax.ppermute(value, 'seq', [(i, i ^ bit) for i in range(RANKS)])  41 us
    ppermute x8, waiting for transfers between devices, along_tensor(): return lax.ppermute(value, 'tensor', pairs)  30.5 us
    pallas_call x2, Pallas kernels, attend(): pl.pallas_call(functools.partial(forward_kernel, heads, per, offset), gri...  22.5 us
    pallas_call x1, Pallas kernels, project(): pl.pallas_call(functools.partial(project_kernel, heads, per), grid_spec=p...  13.1 us
    ppermute x4, waiting for transfers between devices, swap_dp(): return lax.ppermute(value, 'dp', [(0, 1), (1, 0)])  11.8 us
  transfers between devices with their start and end apart: 50, of which 14 were waited for; matrix products, arithmetic and copies ran while one was open for 16% of the time, Pallas kernels for 35%

profile of v1, /device:TPU:0, one launch (start us, length us, event | category | flops | bytes accessed | tf_op | source)
XLA Modules:
  0.0 411.6 jit_solution(1088950538326143651)
XLA Ops:
  7.3 2.3 dynamic-slice_bitcast_fusion
  10.4 1.5 collective-permute-start.3
  11.9 4.9 %collective-permute-start.1 = (bf16[512,768]{1,0:T(8,128)(2,1)}, bf16[512,768]{1,0:T(8,128)(2,1)}, u32[]{:S(2)}, u32[]{:S(2)}) collective-permute-start(bf16[512,768]{1,0:T(8,128)(2,1)} %get-tuple-element.377.x0), channel_id=1, source_target_pairs={{0,8},{4,12},{8,0},{12,4},{1,9},{5,13},{9,1},{13,5},{2,10},{6,14},... | collective-permute-start | bytes 2359304 | tf_op jit(solution)/shard_map/ppermute | solution.py:640
  19.4 1.6 collective-permute-start.4
  21.0 2.2 pad_maximum_fusion.2
  23.7 1.7 collective-permute-start.6
  26.0 2.2 bitcast_select_fusion
  28.2 6.5 %collective-permute-done.1.x2 = bf16[512,768]{1,0:T(8,128)(2,1)} collective-permute-done((bf16[512,768]{1,0:T(8,128)(2,1)}, bf16[512,768]{1,0:T(8,128)(2,1)}, u32[]{:S(2)}, u32[]{:S(2)}) %collective-permute-start.1) | collective-permute-done | bytes 786464 | tf_op jit(solution)/shard_map/ppermute | solution.py:640
  34.7 5.5 %collective-permute-start.2 = (bf16[512,768]{1,0:T(8,128)(2,1)}, bf16[512,768]{1,0:T(8,128)(2,1)}, u32[]{:S(2)}, u32[]{:S(2)}) collective-permute-start(bf16[512,768]{1,0:T(8,128)(2,1)} %collective-permute-done.1.x2), channel_id=1, source_target_pairs={{0,4},{4,0},{8,12},{12,8},{1,5},{5,1},{9,13},{13,9},{2,6},{6,2},{1... | collective-permute-start | bytes 2359304 | tf_op jit(solution)/shard_map/ppermute | solution.py:640
  41.5 4.9 %collective-permute-start.5 = (bf16[512,768]{1,0:T(8,128)(2,1)S(1)}, bf16[512,768]{1,0:T(8,128)(2,1)}, u32[]{:S(2)}, u32[]{:S(2)}) collective-permute-start(bf16[512,768]{1,0:T(8,128)(2,1)S(1)} %get-tuple-element.179.c0), channel_id=1, source_target_pairs={{0,8},{4,12},{8,0},{12,4},{1,9},{5,13},{9,1},{13,5},{2,10},{6,14},... | collective-permute-start | bytes 2359304 | tf_op jit(solution)/shard_map/ppermute | solution.py:640
  46.4 1.4 broadcast_select_fusion.8
  49.7 1.4 pad.20
  51.8 1.4 fusion.42
  53.2 13.1 %project.1 = (bf16[2048,768]{1,0:T(8,128)(2,1)}, bf16[2048,384]{1,0:T(8,128)(2,1)}, bf16[2048,384]{1,0:T(8,128)(2,1)}, bf16[2048,384]{1,0:T(8,128)(2,1)}, bf16[3...) custom-call(s32[8]{0:T(128)} %pad_add_fusion.info, ...), custom_call_target="tpu_custom_call" | custom-call | flops 37748736 | tf_op jit(solution)/shard_map/project/pallas_call | solution.py:150
  66.3 2.5 broadcast_select_fusion.3
  69.8 3.2 collective-permute-start.9
  73.0 11.0 %attend.2 = (bf16[1024,192]{1,0:T(8,128)(2,1)}, f32[192,1024]{1,0:T(8,128)}, f32[8,1024]{1,0:T(8,128)}) custom-call(bf16[2048,384]{1,0:T(8,128)(2,1)} %get-tuple-element.184.qa, bf16[2048,384]{1,0:T(8,128)(2,1)} %get-tuple-element.172.ka, bf16[384,2048]{1,0:T(8,128)(2,1)} %get-tuple-element.173.vt, f32[3,3,128,128]{3,2,1,0:T(8,128)} %get-tuple-element.174.near), custom_call_target="tpu_custom_call" | custom-call | flops 125829120 | tf_op jit(solution)/shard_map/attend/pallas_call | solution.py:236
  84.7 1.3 collective-permute-start.12
  86.8 11.5 %attend.3 = (bf16[1024,192]{1,0:T(8,128)(2,1)}, f32[192,1024]{1,0:T(8,128)}, f32[8,1024]{1,0:T(8,128)}) custom-call(bf16[2048,384]{1,0:T(8,128)(2,1)} %get-tuple-element.184.qa, bf16[2048,384]{1,0:T(8,128)(2,1)} %get-tuple-element.172.ka, bf16[384,2048]{1,0:T(8,128)(2,1)} %get-tuple-element.173.vt, f32[3,3,128,128]{3,2,1,0:T(8,128)} %get-tuple-element.174.near), custom_call_target="tpu_custom_call" | custom-call | flops 125829120 | tf_op jit(solution)/shard_map/attend/pallas_call | solution.py:236
  98.3 1.4 collective-permute-done.11.m2
  99.7 9.5 %collective-permute-done.12.m3 = bf16[1024,192]{1,0:T(8,128)(2,1)} collective-permute-done((bf16[1024,192]{1,0:T(8,128)(2,1)}, bf16[1024,192]{1,0:T(8,128)(2,1)}, u32[]{:S(2)}, u32[]{:S(2)}) %collective-permute-start.12) | collective-permute-done | bytes 393248 | tf_op jit(solution)/shard_map/ppermute | solution.py:640
  111.3 1.8 broadcast_select_fusion.1
  113.1 1.6 pad_maximum_fusion.w_ffn
  114.7 20.5 %middle.2 = (bf16[2,256,768]{2,1,0:T(8,128)(2,1)}, bf16[2,256,768]{2,1,0:T(8,128)(2,1)}, bf16[2,256,768]{2,1,0:T(8,128)(2,1)}, bf16[2,256,768]{2,1,0:T(8,128)(2,...) custom-call(s32[8]{0:T(128)} %pad_add_fusion.info, bf16[512,768]{1,0:T(8,128)(2,1)} %get-tuple-element.377.x0, ...), custom_call_target="tpu_custom_call" | custom-call | flops 188743680 | tf_op jit(solution)/shard_map/middle/pallas_call | solution.py:319
  136.2 1.9 collective-permute-done.19
  139.8 21.2 %middle.3 = (bf16[2,256,768]{2,1,0:T(8,128)(2,1)}, bf16[2,256,768]{2,1,0:T(8,128)(2,1)}, bf16[2,256,768]{2,1,0:T(8,128)(2,1)}, bf16[2,256,768]{2,1,0:T(8,128)(2,...) custom-call(s32[8]{0:T(128)} %pad_add_fusion.info, bf16[512,768]{1,0:T(8,128)(2,1)} %get-tuple-element.377.x0, ...), custom_call_target="tpu_custom_call" | custom-call | flops 188743680 | tf_op jit(solution)/shard_map/middle/pallas_call | solution.py:319
  162.0 2.4 collective-permute-done.22
  168.1 1.8 collective-permute-start.25
  174.4 27.8 %attend_back.2 = (bf16[1024,384]{1,0:T(8,128)(2,1)}, f32[2048,384]{1,0:T(8,128)}, f32[2048,384]{1,0:T(8,128)}, f32[3,3,128,128]{3,2,1,0:T(8,128)}, f32[192,768]{1,0:T(8,128)}, /*index=5*/f32[3,16,128]{2,1,0:T(8,128)}) custom-call(s32[8]{0:T(128)} %pad_add_fusion.info, bf16[2048,384]{1,0:T(8,128)(2,1)} %get-tuple-element.184.qa, ...), custom_call_target="tpu_custom_call" | custom-call | flops 251658240 | tf_op jit(solution)/shard_map/attend_back/pallas_call | solution.py:462
  202.2 2.7 collective-permute-done.26
  204.9 2.0 collective-permute-start.28
  207.0 1.6 add_convert_fusion.2.sum_mine
  211.7 3.3 fusion.15
  216.0 27.6 %attend_back.3 = (bf16[1024,384]{1,0:T(8,128)(2,1)}, bf16[2048,384]{1,0:T(8,128)(2,1)}, bf16[2048,384]{1,0:T(8,128)(2,1)}, f32[3,3,128,128]{3,2,1,0:T(8,128)}, f...) custom-call(s32[8]{0:T(128)} %pad_add_fusion.info, bf16[2048,384]{1,0:T(8,128)(2,1)} %get-tuple-element.184.qa, ...), custom_call_target="tpu_custom_call" | custom-call | flops 251658240 | tf_op jit(solution)/shard_map/attend_back/pallas_call | solution.py:462
  243.6 1.4 broadcast_select_fusion.2
  245.0 9.9 %tail.1 = (bf16[4,256,768]{2,1,0:T(8,128)(2,1)}, bf16[4,256,768]{2,1,0:T(8,128)(2,1)}) custom-call(s32[8]{0:T(128)} %pad_add_fusion.info, bf16[1024,384]{1,0:T(8,128)(2,1)} %get-tuple-element.280.dq0, bf16[1024,384]{1,0:T(8,128)(2,1)} %get-tuple-element.281.dq1, bf16[2048,384]{1,0:T(8,128)(2,1)} %get-tuple-element.282.dk, ...), custom_call_target="tpu_custom_call" | custom-call | flops 56623104 | tf_op jit(solution)/shard_map/tail/pallas_call | solution.py:560
  260.9 3.2 bucket_sums.1
  264.1 1.4 select_reduce_fusion.1
  265.5 2.6 add_convert_fusion.1
  268.1 4.8 %collective-permute-start.31 = (bf16[2,256,768]{2,1,0:T(8,128)(2,1)}, bf16[2,256,768]{2,1,0:T(8,128)(2,1)}, u32[]{:S(2)}, u32[]{:S(2)}) collective-permute-start(bf16[2,256,768]{2,1,0:T(8,128)(2,1)} %add_convert_fusion.1), channel_id=1, source_target_pairs={{0,8},{4,12},{8,0},{12,4},{1,9},{5,13},{9,1},{13,5},{2,10},{6,14},... | collective-permute-start | bytes 2359304 | tf_op jit(solution)/shard_map/ppermute | solution.py:640
  277.8 8.4 %weights.1 = bf16[800,768]{1,0:T(8,128)(2,1)} custom-call(bf16[1024,384]{1,0:T(8,128)(2,1)} %get-tuple-element.280.dq0, bf16[1024,384]{1,0:T(8,128)(2,1)} %get-tuple-element.281.dq1, bf16[2048,384]{1,0:T(8,128)(2,1)} %get-tuple-element.282.dk, bf16[2048,384]{1,0:T(8,128)(2,1)} %get-tuple-element.283.dv, bf16[2048,768]{1,0:T(8,128)(2,1)} %get-tuple-element.170.normed, ...), custom_call_target="tpu_custom_call" | custom-call | flops 56623104 | tf_op jit(solution)/shard_map/weights/pallas_call | solution.py:610
  286.2 2.7 add_convert_fusion
  288.9 2.4 collective-permute-done.31
  291.4 2.2 multiply_reduce_fusion.2
  293.9 2.2 fusion.16
  296.1 1.6 fusion.9
  299.9 1.7 collective-permute-start.36
  301.6 1.9 collective-permute-done.36
  303.5 1.7 collective-permute-start.43
  306.7 1.3 collective-permute-start.32
  308.0 1.6 collective-permute-start.33
  309.6 11.8 %collective-permute-done.34 = bf16[800,384]{1,0:T(8,128)(2,1)} collective-permute-done((bf16[800,384]{1,0:T(8,128)(2,1)}, bf16[800,384]{1,0:T(8,128)(2,1)}, u32[]{:S(2)}, u32[]{:S(2)}) %collective-permute-start.34) | collective-permute-done | bytes 614432 | tf_op jit(solution)/shard_map/ppermute | solution.py:694
  321.4 2.0 add_convert_fusion.7
  323.4 12.7 %collective-permute-done.32 = bf16[512,768]{1,0:T(8,128)(2,1)S(1)} collective-permute-done((bf16[512,768]{1,0:T(8,128)(2,1)}, bf16[512,768]{1,0:T(8,128)(2,1)S(1)}, u32[]{:S(2)}, u32[]{:S(2)}) %collective-permute-start.32) | collective-permute-done | bytes 786464 | tf_op jit(solution)/shard_map/ppermute | solution.py:654
  337.1 2.0 convert_add_fusion
  339.1 1.8 collective-permute-start.41
  343.0 16.5 %collective-permute-start.40 = (bf16[800,384]{1,0:T(8,128)(2,1)S(1)}, bf16[800,384]{1,0:T(8,128)(2,1)S(1)}, u32[]{:S(2)}, u32[]{:S(2)}) collective-permute-start(bf16[800,384]{1,0:T(8,128)(2,1)S(1)} %broadcast_select_fusion.5), channel_id=1, source_target_pairs={{0,4},{4,0},{8,12},{12,8},{1,5},{5,1},{9,13},{13,9},{2,6},{6,2},{1... | collective-permute-start | bytes 1843208 | tf_op jit(solution)/shard_map/ppermute | solution.py:640
  360.0 1.4 copy-done.22
  361.7 1.6 pad_maximum_fusion.1
  363.3 8.9 %collective-permute-done.42 = f32[2,768]{1,0:T(2,128)S(1)} collective-permute-done((f32[2,768]{1,0:T(2,128)S(1)}, f32[2,768]{1,0:T(2,128)S(1)}, u32[]{:S(2)}, u32[]{:S(2)}) %collective-permute-start.42) | collective-permute-done | bytes 6176 | tf_op jit(solution)/shard_map/ppermute | solution.py:654
  373.0 1.6 slice_bitcast_fusion
  377.2 11.2 %collective-permute-done.46 = bf16[800,384]{1,0:T(8,128)(2,1)S(1)} collective-permute-done((bf16[800,384]{1,0:T(8,128)(2,1)S(1)}, bf16[800,384]{1,0:T(8,128)(2,1)S(1)}, u32[]{:S(2)}, u32[]{:S(2)}) %collective-permute-start.46) | collective-permute-done | bytes 614432 | tf_op jit(solution)/shard_map/ppermute | solution.py:640
  388.5 8.9 %collective-permute-done.45 = bf16[512,768]{1,0:T(8,128)(2,1)S(1)} collective-permute-done((bf16[512,768]{1,0:T(8,128)(2,1)S(1)}, bf16[512,768]{1,0:T(8,128)(2,1)S(1)}, u32[]{:S(2)}, u32[]{:S(2)}) %collective-permute-start.45) | collective-permute-done | bytes 786464 | tf_op jit(solution)/shard_map/ppermute | solution.py:654
  399.4 1.4 copy.35
  (273 shorter events, 56.3 us)
Async XLA Ops:
  7.2 197.7 %reduce-scatter.2.cloned.1.call-start = ((), (), s32[]{:S(2)}) async-start(), calls=%async_computation.1 | async-start | bytes 3538944 | tf_op jit(solution)/shard_map/reduce_scatter | solution.py:852
  7.3 10.9 %copy-start.34 = (bf16[768,384]{1,0:T(8,128)(2,1)S(1)}, bf16[768,384]{1,0:T(8,128)(2,1)}, u32[]{:S(2)}) copy-start(bf16[768,384]{1,0:T(8,128)(2,1)} %param.22) | copy-start | bytes 1769476
  10.4 8.9 %collective-permute-start.3 = (bf16[800,384]{1,0:T(8,128)(2,1)S(1)}, bf16[800,384]{1,0:T(8,128)(2,1)}, u32[]{:S(2)}, u32[]{:S(2)}) collective-permute-start(bf16[800,384]{1,0:T(8,128)(2,1)S(1)} %concatenate.37), channel_id=1, source_target_pairs={{4,6},{5,7},{6,4},{7,5},{8,9},{9,8},{10,11},{11,10},{12,15},{13,14... | collective-permute-start | bytes 1843208 | tf_op jit(solution)/shard_map/ppermute | solution.py:649
  11.9 22.8 %collective-permute-start.1 = (bf16[512,768]{1,0:T(8,128)(2,1)}, bf16[512,768]{1,0:T(8,128)(2,1)}, u32[]{:S(2)}, u32[]{:S(2)}) collective-permute-start(bf16[512,768]{1,0:T(8,128)(2,1)} %get-tuple-element.377.x0), channel_id=1, source_target_pairs={{0,8},{4,12},{8,0},{12,4},{1,9},{5,13},{9,1},{13,5},{2,10},{6,14},... | collective-permute-start | bytes 2359304 | tf_op jit(solution)/shard_map/ppermute | solution.py:640
  16.9 36.3 %collective-permute-start = (bf16[512,768]{1,0:T(8,128)(2,1)}, bf16[512,768]{1,0:T(8,128)(2,1)}, u32[]{:S(2)}, u32[]{:S(2)}) collective-permute-start(bf16[512,768]{1,0:T(8,128)(2,1)} %get-tuple-element.377.x0), channel_id=1, source_target_pairs={{0,4},{4,0},{8,12},{12,8},{1,5},{5,1},{9,13},{13,9},{2,6},{6,2},{1... | collective-permute-start | bytes 2359304 | tf_op jit(solution)/shard_map/ppermute | solution.py:640
  19.3 8.9 %copy-start.18 = (bf16[800,384]{1,0:T(8,128)(2,1)}, bf16[800,384]{1,0:T(8,128)(2,1)S(1)}, u32[]{:S(2)}) copy-start(bf16[800,384]{1,0:T(8,128)(2,1)S(1)} %broadcast_select_fusion.6) | copy-start | bytes 1843204
  19.4 27.0 %collective-permute-start.4 = (bf16[800,384]{1,0:T(8,128)(2,1)S(1)}, bf16[800,384]{1,0:T(8,128)(2,1)}, u32[]{:S(2)}, u32[]{:S(2)}) collective-permute-start(bf16[800,384]{1,0:T(8,128)(2,1)S(1)} %broadcast_select_fusion.6), channel_id=1, source_target_pairs={{0,16},{16,0},{1,17},{17,1},{2,18},{18,2},{3,19},{19,3},{4,20},{20... | collective-permute-start | bytes 1843208 | tf_op jit(solution)/shard_map/ppermute | solution.py:694
  23.7 42.5 %collective-permute-start.6 = (bf16[384,1536]{1,0:T(8,128)(2,1)}, bf16[384,1536]{1,0:T(8,128)(2,1)}, u32[]{:S(2)}, u32[]{:S(2)}) collective-permute-start(bf16[384,1536]{1,0:T(8,128)(2,1)} %pad_maximum_fusion.2), channel_id=1, source_target_pairs={{4,6},{5,7},{6,4},{7,5},{8,9},{9,8},{10,11},{11,10},{12,15},{13,14... | collective-permute-start | bytes 3538952 | tf_op jit(solution)/shard_map/ppermute | solution.py:649
  28.2 20.4 %copy-start = (bf16[512,768]{1,0:T(8,128)(2,1)}, bf16[512,768]{1,0:T(8,128)(2,1)S(1)}, u32[]{:S(2)}) copy-start(bf16[512,768]{1,0:T(8,128)(2,1)S(1)} %get-tuple-element.179.c0) | copy-start | bytes 2359300
  34.7 18.5 %collective-permute-start.2 = (bf16[512,768]{1,0:T(8,128)(2,1)}, bf16[512,768]{1,0:T(8,128)(2,1)}, u32[]{:S(2)}, u32[]{:S(2)}) collective-permute-start(bf16[512,768]{1,0:T(8,128)(2,1)} %collective-permute-done.1.x2), channel_id=1, source_target_pairs={{0,4},{4,0},{8,12},{12,8},{1,5},{5,1},{9,13},{13,9},{2,6},{6,2},{1... | collective-permute-start | bytes 2359304 | tf_op jit(solution)/shard_map/ppermute | solution.py:640
  41.5 27.2 %collective-permute-start.5 = (bf16[512,768]{1,0:T(8,128)(2,1)S(1)}, bf16[512,768]{1,0:T(8,128)(2,1)}, u32[]{:S(2)}, u32[]{:S(2)}) collective-permute-start(bf16[512,768]{1,0:T(8,128)(2,1)S(1)} %get-tuple-element.179.c0), channel_id=1, source_target_pairs={{0,8},{4,12},{8,0},{12,4},{1,9},{5,13},{9,1},{13,5},{2,10},{6,14},... | collective-permute-start | bytes 2359304 | tf_op jit(solution)/shard_map/ppermute | solution.py:640
  46.4 37.6 %collective-permute-start.7 = (bf16[512,768]{1,0:T(8,128)(2,1)S(1)}, bf16[512,768]{1,0:T(8,128)(2,1)}, u32[]{:S(2)}, u32[]{:S(2)}) collective-permute-start(bf16[512,768]{1,0:T(8,128)(2,1)S(1)} %get-tuple-element.179.c0), channel_id=1, source_target_pairs={{0,4},{4,0},{8,12},{12,8},{1,5},{5,1},{9,13},{13,9},{2,6},{6,2},{1... | collective-permute-start | bytes 2359304 | tf_op jit(solution)/shard_map/ppermute | solution.py:640
  68.7 15.3 %collective-permute-start.8 = (bf16[512,768]{1,0:T(8,128)(2,1)}, bf16[512,768]{1,0:T(8,128)(2,1)}, u32[]{:S(2)}, u32[]{:S(2)}) collective-permute-start(bf16[512,768]{1,0:T(8,128)(2,1)} %collective-permute-done.5.c2), channel_id=1, source_target_pairs={{0,4},{4,0},{8,12},{12,8},{1,5},{5,1},{9,13},{13,9},{2,6},{6,2},{1... | collective-permute-start | bytes 2359304 | tf_op jit(solution)/shard_map/ppermute | solution.py:640
  69.3 39.9 %collective-permute-start.15 = (bf16[384,1536]{1,0:T(8,128)(2,1)}, bf16[384,1536]{1,0:T(8,128)(2,1)}, u32[]{:S(2)}, u32[]{:S(2)}) collective-permute-start(bf16[384,1536]{1,0:T(8,128)(2,1)} %broadcast_select_fusion.3), channel_id=1, source_target_pairs={{0,16},{16,0},{1,17},{17,1},{2,18},{18,2},{3,19},{19,3},{4,20},{20... | collective-permute-start | bytes 3538952 | tf_op jit(solution)/shard_map/ppermute | solution.py:694
  69.8 14.2 %copy-start.13 = (bf16[192,768]{1,0:T(8,128)(2,1)}, bf16[192,768]{1,0:T(8,128)(2,1)S(1)}, u32[]{:S(2)}) copy-start(bf16[192,768]{1,0:T(8,128)(2,1)S(1)} %fusion.29.w0) | copy-start | bytes 884740
  69.8 14.2 %collective-permute-start.9 = (bf16[192,768]{1,0:T(8,128)(2,1)S(1)}, bf16[192,768]{1,0:T(8,128)(2,1)S(1)}, u32[]{:S(2)}, u32[]{:S(2)}) collective-permute-start(bf16[192,768]{1,0:T(8,128)(2,1)S(1)} %fusion.29.w0), channel_id=1, source_target_pairs={{0,8},{4,12},{8,0},{12,4},{1,9},{5,13},{9,1},{13,5},{2,10},{6,14},... | collective-permute-start | bytes 884744 | tf_op jit(solution)/shard_map/ppermute | solution.py:640
  73.0 13.1 %collective-permute-start.13 = (bf16[192,768]{1,0:T(8,128)(2,1)S(1)}, bf16[192,768]{1,0:T(8,128)(2,1)S(1)}, u32[]{:S(2)}, u32[]{:S(2)}) collective-permute-start(bf16[192,768]{1,0:T(8,128)(2,1)S(1)} %fusion.29.w0), channel_id=1, source_target_pairs={{0,4},{4,0},{8,12},{12,8},{1,5},{5,1},{9,13},{13,9},{2,6},{6,2},{1... | collective-permute-start | bytes 884744 | tf_op jit(solution)/shard_map/ppermute | solution.py:640
  84.0 14.2 %copy-start.23 = (bf16[192,768]{1,0:T(8,128)(2,1)}, bf16[192,768]{1,0:T(8,128)(2,1)S(1)}, u32[]{:S(2)}) copy-start(bf16[192,768]{1,0:T(8,128)(2,1)S(1)} %collective-permute-done.9.w2) | copy-start | bytes 884740
  84.0 14.2 %collective-permute-start.10 = (bf16[1024,192]{1,0:T(8,128)(2,1)}, bf16[1024,192]{1,0:T(8,128)(2,1)S(1)}, u32[]{:S(2)}, u32[]{:S(2)}) collective-permute-start(bf16[1024,192]{1,0:T(8,128)(2,1)} %get-tuple-element.190.m0), channel_id=1, source_target_pairs={{0,4},{4,0},{8,12},{12,8},{1,5},{5,1},{9,13},{13,9},{2,6},{6,2},{1... | collective-permute-start | bytes 1179656 | tf_op jit(solution)/shard_map/ppermute | solution.py:640
  84.6 15.1 %collective-permute-start.11 = (bf16[1024,192]{1,0:T(8,128)(2,1)}, bf16[1024,192]{1,0:T(8,128)(2,1)}, u32[]{:S(2)}, u32[]{:S(2)}) collective-permute-start(bf16[1024,192]{1,0:T(8,128)(2,1)} %get-tuple-element.190.m0), channel_id=1, source_target_pairs={{0,8},{4,12},{8,0},{12,4},{1,9},{5,13},{9,1},{13,5},{2,10},{6,14},... | collective-permute-start | bytes 1179656 | tf_op jit(solution)/shard_map/ppermute | solution.py:640
  84.7 24.5 %collective-permute-start.12 = (bf16[1024,192]{1,0:T(8,128)(2,1)}, bf16[1024,192]{1,0:T(8,128)(2,1)}, u32[]{:S(2)}, u32[]{:S(2)}) collective-permute-start(bf16[1024,192]{1,0:T(8,128)(2,1)} %get-tuple-element.190.m0), channel_id=1, source_target_pairs={{0,12},{4,8},{8,4},{12,0},{1,13},{5,9},{9,5},{13,1},{2,14},{6,10},... | collective-permute-start | bytes 1179656 | tf_op jit(solution)/shard_map/ppermute | solution.py:640
  86.0 12.2 %copy-start.24 = (bf16[192,768]{1,0:T(8,128)(2,1)}, bf16[192,768]{1,0:T(8,128)(2,1)S(1)}, u32[]{:S(2)}) copy-start(bf16[192,768]{1,0:T(8,128)(2,1)S(1)} %collective-permute-done.13.w1) | copy-start | bytes 884740
  86.1 12.2 %collective-permute-start.14 = (bf16[192,768]{1,0:T(8,128)(2,1)S(1)}, bf16[192,768]{1,0:T(8,128)(2,1)S(1)}, u32[]{:S(2)}, u32[]{:S(2)}) collective-permute-start(bf16[192,768]{1,0:T(8,128)(2,1)S(1)} %collective-permute-done.9.w2), channel_id=1, source_target_pairs={{0,4},{4,0},{8,12},{12,8},{1,5},{5,1},{9,13},{13,9},{2,6},{6,2},{1... | collective-permute-start | bytes 884744 | tf_op jit(solution)/shard_map/ppermute | solution.py:640
  98.3 14.8 %copy-start.25 = (bf16[192,768]{1,0:T(8,128)(2,1)}, bf16[192,768]{1,0:T(8,128)(2,1)S(1)}, u32[]{:S(2)}) copy-start(bf16[192,768]{1,0:T(8,128)(2,1)S(1)} %collective-permute-done.14.w3) | copy-start | bytes 884740
  98.3 10.9 %copy-start.38 = (bf16[1024,192]{1,0:T(8,128)(2,1)}, bf16[1024,192]{1,0:T(8,128)(2,1)S(1)}, u32[]{:S(2)}) copy-start(bf16[1024,192]{1,0:T(8,128)(2,1)S(1)} %collective-permute-done.10.m1) | copy-start | bytes 1179652
  109.2 26.0 %collective-permute-start.16 = (bf16[1024,192]{1,0:T(8,128)(2,1)}, bf16[1024,192]{1,0:T(8,128)(2,1)S(1)}, u32[]{:S(2)}, u32[]{:S(2)}) collective-permute-start(bf16[1024,192]{1,0:T(8,128)(2,1)} %get-tuple-element.214.m0), channel_id=1, source_target_pairs={{0,4},{4,0},{8,12},{12,8},{1,5},{5,1},{9,13},{13,9},{2,6},{6,2},{1... | collective-permute-start | bytes 1179656 | tf_op jit(solution)/shard_map/ppermute | solution.py:640
  109.9 25.3 %collective-permute-start.17 = (bf16[1024,192]{1,0:T(8,128)(2,1)}, bf16[1024,192]{1,0:T(8,128)(2,1)S(1)}, u32[]{:S(2)}, u32[]{:S(2)}) collective-permute-start(bf16[1024,192]{1,0:T(8,128)(2,1)} %get-tuple-element.214.m0), channel_id=1, source_target_pairs={{0,8},{4,12},{8,0},{12,4},{1,9},{5,13},{9,1},{13,5},{2,10},{6,14},... | collective-permute-start | bytes 1179656 | tf_op jit(solution)/shard_map/ppermute | solution.py:640
  110.2 25.0 %collective-permute-start.18 = (bf16[1024,192]{1,0:T(8,128)(2,1)}, bf16[1024,192]{1,0:T(8,128)(2,1)S(1)}, u32[]{:S(2)}, u32[]{:S(2)}) collective-permute-start(bf16[1024,192]{1,0:T(8,128)(2,1)} %get-tuple-element.214.m0), channel_id=1, source_target_pairs={{0,12},{4,8},{8,4},{12,0},{1,13},{5,9},{9,5},{13,1},{2,14},{6,10},... | collective-permute-start | bytes 1179656 | tf_op jit(solution)/shard_map/ppermute | solution.py:640
  135.2 2.9 collective-permute-start.19
  139.4 21.6 %collective-permute-start.20 = (bf16[2,256,768]{2,1,0:T(8,128)(2,1)S(1)}, bf16[2,256,768]{2,1,0:T(8,128)(2,1)S(1)}, u32[]{:S(2)}, u32[]{:S(2)}) collective-permute-start(bf16[2,256,768]{2,1,0:T(8,128)(2,1)S(1)} %add_convert_fusion.5), channel_id=1, source_target_pairs={{0,8},{4,12},{8,0},{12,4},{1,9},{5,13},{9,1},{13,5},{2,10},{6,14},... | collective-permute-start | bytes 2359304 | tf_op jit(solution)/shard_map/ppermute | solution.py:640
  161.9 2.5 collective-permute-start.22
  165.8 170.4 %all-gather.3.cloned.1.call-start = ((), (), s32[]{:S(2)}) async-start(), calls=%async_computation.2 | async-start | bytes 3932160 | tf_op jit(solution)/shard_map/all_gather | solution.py:877
  166.0 3.9 collective-permute-start.23
  166.2 4.0 collective-permute-start.24
  167.9 5.6 %collective-permute-start.21 = (bf16[2,256,768]{2,1,0:T(8,128)(2,1)S(1)}, bf16[2,256,768]{2,1,0:T(8,128)(2,1)S(1)}, u32[]{:S(2)}, u32[]{:S(2)}) collective-permute-start(bf16[2,256,768]{2,1,0:T(8,128)(2,1)S(1)} %add_convert_fusion.4.sum_mine), channel_id=1, source_target_pairs={{0,4},{4,0},{8,12},{12,8},{1,5},{5,1},{9,13},{13,9},{2,6},{6,2},{1... | collective-permute-start | bytes 2359304 | tf_op jit(solution)/shard_map/ppermute | solution.py:640
  168.1 34.1 %collective-permute-start.25 = (bf16[2,256,768]{2,1,0:T(8,128)(2,1)S(1)}, bf16[2,256,768]{2,1,0:T(8,128)(2,1)}, u32[]{:S(2)}, u32[]{:S(2)}) collective-permute-start(bf16[2,256,768]{2,1,0:T(8,128)(2,1)S(1)} %add_convert_fusion.3), channel_id=1, source_target_pairs={{0,8},{4,12},{8,0},{12,4},{1,9},{5,13},{9,1},{13,5},{2,10},{6,14},... | collective-permute-start | bytes 2359304 | tf_op jit(solution)/shard_map/ppermute | solution.py:640
  172.2 32.7 %collective-permute-start.26 = (bf16[2,256,768]{2,1,0:T(8,128)(2,1)}, bf16[2,256,768]{2,1,0:T(8,128)(2,1)}, u32[]{:S(2)}, u32[]{:S(2)}) collective-permute-start(bf16[2,256,768]{2,1,0:T(8,128)(2,1)} %pad_maximum_fusion.3), channel_id=1, source_target_pairs={{0,8},{4,12},{8,0},{12,4},{1,9},{5,13},{9,1},{13,5},{2,10},{6,14},... | collective-permute-start | bytes 2359304 | tf_op jit(solution)/shard_map/ppermute | solution.py:640
  204.9 38.6 %collective-permute-start.28 = (bf16[384,1536]{1,0:T(8,128)(2,1)}, bf16[384,1536]{1,0:T(8,128)(2,1)}, u32[]{:S(2)}, u32[]{:S(2)}) collective-permute-start(bf16[384,1536]{1,0:T(8,128)(2,1)} %reduce-scatter.2.cloned.1.call-done), channel_id=1, source_target_pairs={{4,6},{6,4},{7,5},{8,9},{10,11},{11,10},{12,15},{14,13},{15,12},{2... | collective-permute-start | bytes 3538952 | tf_op jit(solution)/shard_map/ppermute | solution.py:649
  208.5 7.5 %collective-permute-start.27 = (bf16[2,256,768]{2,1,0:T(8,128)(2,1)S(1)}, bf16[2,256,768]{2,1,0:T(8,128)(2,1)}, u32[]{:S(2)}, u32[]{:S(2)}) collective-permute-start(bf16[2,256,768]{2,1,0:T(8,128)(2,1)S(1)} %add_convert_fusion.2.sum_mine), channel_id=1, source_target_pairs={{0,4},{4,0},{8,12},{12,8},{1,5},{5,1},{9,13},{13,9},{2,6},{6,2},{1... | collective-permute-start | bytes 2359304 | tf_op jit(solution)/shard_map/ppermute | solution.py:640
  254.9 10.7 %collective-permute-start.29 = (bf16[4,256,768]{2,1,0:T(8,128)(2,1)}, bf16[4,256,768]{2,1,0:T(8,128)(2,1)}, u32[]{:S(2)}, u32[]{:S(2)}) collective-permute-start(bf16[4,256,768]{2,1,0:T(8,128)(2,1)} %get-tuple-element.274), channel_id=1, source_target_pairs={{0,4},{4,0},{8,12},{12,8},{1,5},{5,1},{9,13},{13,9},{2,6},{6,2},{1... | collective-permute-start | bytes 4718600 | tf_op jit(solution)/shard_map/ppermute | solution.py:640
  255.6 10.0 %collective-permute-start.30 = (bf16[384,1536]{1,0:T(8,128)(2,1)S(1)}, bf16[384,1536]{1,0:T(8,128)(2,1)}, u32[]{:S(2)}, u32[]{:S(2)}) collective-permute-start(bf16[384,1536]{1,0:T(8,128)(2,1)S(1)} %broadcast_select_fusion.2), channel_id=1, source_target_pairs={{0,4},{4,0},{8,12},{12,8},{1,5},{5,1},{9,13},{13,9},{2,6},{6,2},{1... | collective-permute-start | bytes 3538952 | tf_op jit(solution)/shard_map/ppermute | solution.py:640
  265.5 8.3 %copy-start.51 = (f32[3]{0:T(128)S(1)}, f32[3]{0:T(128)}, u32[]{:S(2)}) copy-start(f32[3]{0:T(128)} %get-tuple-element.358) | copy-start | bytes 40
  268.1 23.2 %collective-permute-start.31 = (bf16[2,256,768]{2,1,0:T(8,128)(2,1)}, bf16[2,256,768]{2,1,0:T(8,128)(2,1)}, u32[]{:S(2)}, u32[]{:S(2)}) collective-permute-start(bf16[2,256,768]{2,1,0:T(8,128)(2,1)} %add_convert_fusion.1), channel_id=1, source_target_pairs={{0,8},{4,12},{8,0},{12,4},{1,9},{5,13},{9,1},{13,5},{2,10},{6,14},... | collective-permute-start | bytes 2359304 | tf_op jit(solution)/shard_map/ppermute | solution.py:640
  286.2 7.4 %copy-start.8 = (f32[2,256,768]{2,1,0:T(8,128)S(1)}, f32[2,256,768]{2,1,0:T(8,128)}, u32[]{:S(2)}) copy-start(f32[2,256,768]{2,1,0:T(8,128)} %select_convert_fusion) | copy-start | bytes 4718596
  297.8 7.5 %copy-start.9 = (bf16[800,768]{1,0:T(8,128)(2,1)S(1)}, bf16[800,768]{1,0:T(8,128)(2,1)}, u32[]{:S(2)}) copy-start(bf16[800,768]{1,0:T(8,128)(2,1)} %weights.1) | copy-start | bytes 3686404
  298.7 1.2 collective-permute-start.35
  299.9 3.6 collective-permute-start.36
  303.5 33.5 %collective-permute-start.43 = (bf16[384,1536]{1,0:T(8,128)(2,1)}, bf16[384,1536]{1,0:T(8,128)(2,1)}, u32[]{:S(2)}, u32[]{:S(2)}) collective-permute-start(bf16[384,1536]{1,0:T(8,128)(2,1)} %add_convert_fusion), channel_id=1, source_target_pairs={{0,8},{4,12},{8,0},{12,4},{1,9},{5,13},{9,1},{13,5},{2,10},{6,14},... | collective-permute-start | bytes 3538952 | tf_op jit(solution)/shard_map/ppermute | solution.py:640
  306.2 15.2 %collective-permute-start.34 = (bf16[800,384]{1,0:T(8,128)(2,1)}, bf16[800,384]{1,0:T(8,128)(2,1)}, u32[]{:S(2)}, u32[]{:S(2)}) collective-permute-start(bf16[800,384]{1,0:T(8,128)(2,1)} %constant_dynamic-slice_fusion.1), channel_id=1, source_target_pairs={{0,16},{16,0},{1,17},{17,1},{2,18},{18,2},{3,19},{19,3},{4,20},{20... | collective-permute-start | bytes 1843208 | tf_op jit(solution)/shard_map/ppermute | solution.py:694
  306.7 29.4 %collective-permute-start.32 = (bf16[512,768]{1,0:T(8,128)(2,1)}, bf16[512,768]{1,0:T(8,128)(2,1)S(1)}, u32[]{:S(2)}, u32[]{:S(2)}) collective-permute-start(bf16[512,768]{1,0:T(8,128)(2,1)} %pad_maximum_fusion.5), channel_id=1, source_target_pairs={{0,1},{2,3},{4,5},{6,7},{8,9},{10,11},{12,13},{14,15},{16,17},{18,... | collective-permute-start | bytes 2359304 | tf_op jit(solution)/shard_map/ppermute | solution.py:654
  308.0 28.1 %collective-permute-start.33 = (bf16[512,768]{1,0:T(8,128)(2,1)}, bf16[512,768]{1,0:T(8,128)(2,1)}, u32[]{:S(2)}, u32[]{:S(2)}) collective-permute-start(bf16[512,768]{1,0:T(8,128)(2,1)} %pad_maximum_fusion.5), channel_id=1, source_target_pairs={{3,2},{2,1},{7,6},{6,5},{11,10},{10,9},{15,14},{14,13},{19,18},{18... | collective-permute-start | bytes 2359304 | tf_op jit(solution)/shard_map/ppermute | solution.py:654
  336.1 6.8 %collective-permute-start.39 = (bf16[800,384]{1,0:T(8,128)(2,1)}, bf16[800,384]{1,0:T(8,128)(2,1)S(1)}, u32[]{:S(2)}, u32[]{:S(2)}) collective-permute-start(bf16[800,384]{1,0:T(8,128)(2,1)} %add_convert_fusion.7), channel_id=1, source_target_pairs={{4,6},{6,4},{7,5},{8,9},{10,11},{11,10},{12,15},{14,13},{15,12},{2... | collective-permute-start | bytes 1843208 | tf_op jit(solution)/shard_map/ppermute | solution.py:649
  339.1 22.5 %collective-permute-start.41 = (f32[2,768]{1,0:T(2,128)S(1)}, f32[2,768]{1,0:T(2,128)S(1)}, u32[]{:S(2)}, u32[]{:S(2)}) collective-permute-start(f32[2,768]{1,0:T(2,128)S(1)} %add.384), channel_id=1, source_target_pairs={{0,16},{16,0},{1,17},{17,1},{2,18},{18,2},{3,19},{19,3},{4,20},{20... | collective-permute-start | bytes 18440 | tf_op jit(solution)/shard_map/ppermute | solution.py:694
  340.9 31.5 %collective-permute-start.37 = (bf16[512,768]{1,0:T(8,128)(2,1)S(1)}, bf16[512,768]{1,0:T(8,128)(2,1)S(1)}, u32[]{:S(2)}, u32[]{:S(2)}) collective-permute-start(bf16[512,768]{1,0:T(8,128)(2,1)S(1)} %collective-permute-done.32), channel_id=1, source_target_pairs={{1,2},{5,6},{9,10},{13,14},{17,18},{21,22},{25,26},{29,30}} | collective-permute-start | bytes 2359304 | tf_op jit(solution)/shard_map/ppermute | solution.py:654
  341.6 30.8 %collective-permute-start.38 = (bf16[512,768]{1,0:T(8,128)(2,1)}, bf16[512,768]{1,0:T(8,128)(2,1)S(1)}, u32[]{:S(2)}, u32[]{:S(2)}) collective-permute-start(bf16[512,768]{1,0:T(8,128)(2,1)} %collective-permute-done.33), channel_id=1, source_target_pairs={{2,1},{1,0},{6,5},{5,4},{10,9},{9,8},{14,13},{13,12},{18,17},{17,1... | collective-permute-start | bytes 2359304 | tf_op jit(solution)/shard_map/ppermute | solution.py:654
  343.0 29.2 %collective-permute-start.40 = (bf16[800,384]{1,0:T(8,128)(2,1)S(1)}, bf16[800,384]{1,0:T(8,128)(2,1)S(1)}, u32[]{:S(2)}, u32[]{:S(2)}) collective-permute-start(bf16[800,384]{1,0:T(8,128)(2,1)S(1)} %broadcast_select_fusion.5), channel_id=1, source_target_pairs={{0,4},{4,0},{8,12},{12,8},{1,5},{5,1},{9,13},{13,9},{2,6},{6,2},{1... | collective-permute-start | bytes 1843208 | tf_op jit(solution)/shard_map/ppermute | solution.py:640
  361.6 10.6 %collective-permute-start.42 = (f32[2,768]{1,0:T(2,128)S(1)}, f32[2,768]{1,0:T(2,128)S(1)}, u32[]{:S(2)}, u32[]{:S(2)}) collective-permute-start(f32[2,768]{1,0:T(2,128)S(1)} %add.386), channel_id=1, source_target_pairs={{0,1},{1,0},{2,3},{3,2},{4,5},{5,4},{6,7},{7,6},{8,9},{9,8},{10,11... | collective-permute-start | bytes 18440 | tf_op jit(solution)/shard_map/ppermute | solution.py:654
  372.4 4.8 %collective-permute-start.47 = (f32[2,768]{1,0:T(2,128)S(1)}, f32[2,768]{1,0:T(2,128)S(1)}, u32[]{:S(2)}, u32[]{:S(2)}) collective-permute-start(f32[2,768]{1,0:T(2,128)S(1)} %add.387), channel_id=1, source_target_pairs={{0,2},{1,3},{2,0},{3,1},{4,6},{5,7},{6,4},{7,5},{8,10},{9,11},{10,... | collective-permute-start | bytes 18440 | tf_op jit(solution)/shard_map/ppermute | solution.py:654
  372.5 15.9 %collective-permute-start.46 = (bf16[800,384]{1,0:T(8,128)(2,1)S(1)}, bf16[800,384]{1,0:T(8,128)(2,1)S(1)}, u32[]{:S(2)}, u32[]{:S(2)}) collective-permute-start(bf16[800,384]{1,0:T(8,128)(2,1)S(1)} %add_convert_fusion.6), channel_id=1, source_target_pairs={{0,8},{4,12},{8,0},{12,4},{1,9},{5,13},{9,1},{13,5},{2,10},{6,14},... | collective-permute-start | bytes 1843208 | tf_op jit(solution)/shard_map/ppermute | solution.py:640
  374.5 14.0 %collective-permute-start.44 = (bf16[512,768]{1,0:T(8,128)(2,1)S(1)}, bf16[512,768]{1,0:T(8,128)(2,1)S(1)}, u32[]{:S(2)}, u32[]{:S(2)}) collective-permute-start(bf16[512,768]{1,0:T(8,128)(2,1)S(1)} %collective-permute-done.37), channel_id=1, source_target_pairs={{2,3},{6,7},{10,11},{14,15},{18,19},{22,23},{26,27},{30,31}} | collective-permute-start | bytes 2359304 | tf_op jit(solution)/shard_map/ppermute | solution.py:654
  375.2 22.2 %collective-permute-start.45 = (bf16[512,768]{1,0:T(8,128)(2,1)S(1)}, bf16[512,768]{1,0:T(8,128)(2,1)S(1)}, u32[]{:S(2)}, u32[]{:S(2)}) collective-permute-start(bf16[512,768]{1,0:T(8,128)(2,1)S(1)} %collective-permute-done.38), channel_id=1, source_target_pairs={{1,0},{5,4},{9,8},{13,12},{17,16},{21,20},{25,24},{29,28}} | collective-permute-start | bytes 2359304 | tf_op jit(solution)/shard_map/ppermute | solution.py:654
  377.2 22.2 %copy-start.20 = (bf16[3,512,768]{2,1,0:T(8,128)(2,1)}, bf16[3,512,768]{2,1,0:T(8,128)(2,1)S(1)}, u32[]{:S(2)}) copy-start(bf16[3,512,768]{2,1,0:T(8,128)(2,1)S(1)} %bitcast_dynamic-update-slice_fusion.2) | copy-start | bytes 7077892
  388.5 10.9 %copy-start.12 = (f32[768,384]{0,1:T(8,128)S(1)}, f32[768,384]{0,1:T(8,128)}, u32[]{:S(2)}) copy-start(f32[768,384]{0,1:T(8,128)} %get-tuple-element.347) | copy-start | bytes 3538948
  388.5 9.8 %copy-start.31 = (bf16[512,768]{1,0:T(8,128)(2,1)}, bf16[512,768]{1,0:T(8,128)(2,1)S(1)}, u32[]{:S(2)}) copy-start(bf16[512,768]{1,0:T(8,128)(2,1)S(1)} %collective-permute-done.44) | copy-start | bytes 2359300
  (44 other events, 117.2 us)
Sparse Core Ops, SparseCore 0:
  165.9 35.6 reduce-scatter.1
  258.0 72.4 all-gather.2

commit v2 on v1

--- a/solution.py
+++ b/solution.py
@@ -88,10 +88,6 @@
     return value
 
 
-def pick_pair(info, chunk, refs):
-    return jnp.concatenate([pick_block(info[chunk + k], refs) for k in range(2)], axis=0)
-
-
 def project_kernel(
     heads, per, info, x0, x1, x2, x3, gain_ref, w_ref, table, normed, qa, ka, va, kt, vt, near
 ):
@@ -107,8 +103,9 @@
                     tile = jnp.where(buckets == b, table[b, h], tile)
                 near[h, d + 1] = tile
 
-    rows = 2 * x0.shape[0]
-    x = pick_pair(info, (2 * step) % RANKS, (x0, x1, x2, x3)).astype(FULL)
+    rows = RANKS * x0.shape[0]
+    refs = (x0, x1, x2, x3)
+    x = jnp.concatenate([pick_block(info[k], refs) for k in range(RANKS)], axis=0).astype(FULL)
     scale = lax.rsqrt(jnp.mean(x * x, axis=-1, keepdims=True) + EPSILON)
     xn = (x * scale * gain_ref[...]).astype(LOW)
     normed[...] = xn
@@ -144,15 +141,15 @@
     total = RANKS * xs[0].shape[0]
     rows = xs[0].shape[0] // SPLIT
     width = xs[0].shape[1]
-    row_block = lambda w: pl.BlockSpec((2 * rows, w), lambda i, c: (i, 0))
-    col_block = lambda w: pl.BlockSpec((w, 2 * rows), lambda i, c: (0, i))
+    row_block = lambda w: pl.BlockSpec((RANKS * rows, w), lambda i, c: (i, 0))
+    col_block = lambda w: pl.BlockSpec((w, RANKS * rows), lambda i, c: (0, i))
     wide = heads * TILE
     return pl.pallas_call(
         functools.partial(project_kernel, heads, per),
         grid_spec=pltpu.PrefetchScalarGridSpec(
             num_scalar_prefetch=1,
-            grid=(RANKS * SPLIT // 2,),
-            in_specs=[pl.BlockSpec((rows, width), lambda i, c: (2 * i // RANKS, 0))] * RANKS
+            grid=(SPLIT,),
+            in_specs=[pl.BlockSpec((rows, width), lambda i, c: (i, 0))] * RANKS
             + [
                 whole_spec(gain.shape),
                 whole_spec(w_qkv.shape),

time: 417 us -> 418 us (level)
  no operation moved by 1% of the time
where the time goes in v2:
time: 418 us; the launch traced here: 412 us
  Pallas kernels  154 us (37%)
  waiting for transfers between devices  83.3 us (20%)
  starting transfers between devices  73.2 us (18%)
  other arithmetic  64.3 us (15%)
  local copies, waits for them, and re-layouts  21.1 us (5%)
  between operations  15.6 us (4%)
    ppermute x32, starting transfers between devices, swap_seq(): return lax.ppermute(value, 'seq', [(i, i ^ bit) for i in range(RANKS)])  55.6 us
    pallas_call x2, Pallas kernels, attend_back(): pl.pallas_call(functools.partial(backward_kernel, per, offset, kc), grid_...  55.4 us
    pallas_call x2, Pallas kernels, middle(): pl.pallas_call(functools.partial(middle_kernel, given is None), grid_spec...  41.7 us
    ppermute x32, waiting for transfers between devices, swap_seq(): return lax.ppermute(value, 'seq', [(i, i ^ bit) for i in range(RANKS)])  41 us
    ppermute x8, waiting for transfers between devices, along_tensor(): return lax.ppermute(value, 'tensor', pairs)  30.5 us
    pallas_call x2, Pallas kernels, attend(): pl.pallas_call(functools.partial(forward_kernel, heads, per, offset), gri...  22.5 us
    pallas_call x1, Pallas kernels, project(): pl.pallas_call(functools.partial(project_kernel, heads, per), grid_spec=p...  13.1 us
    ppermute x4, waiting for transfers between devices, swap_dp(): return lax.ppermute(value, 'dp', [(0, 1), (1, 0)])  11.8 us
  transfers between devices with their start and end apart: 50, of which 14 were waited for; matrix products, arithmetic and copies ran while one was open for 16% of the time, Pallas kernels for 35%

profile of v2, /device:TPU:0, one launch (start us, length us, event | category | flops | bytes accessed | tf_op | source)
XLA Modules:
  0.0 411.6 jit_solution(15298412810244801606)
XLA Ops:
  7.3 2.3 dynamic-slice_bitcast_fusion
  10.4 1.5 collective-permute-start.3
  11.9 4.9 %collective-permute-start.1 = (bf16[512,768]{1,0:T(8,128)(2,1)}, bf16[512,768]{1,0:T(8,128)(2,1)}, u32[]{:S(2)}, u32[]{:S(2)}) collective-permute-start(bf16[512,768]{1,0:T(8,128)(2,1)} %get-tuple-element.377.x0), channel_id=1, source_target_pairs={{0,8},{4,12},{8,0},{12,4},{1,9},{5,13},{9,1},{13,5},{2,10},{6,14},... | collective-permute-start | bytes 2359304 | tf_op jit(solution)/shard_map/ppermute | solution.py:637
  19.4 1.6 collective-permute-start.4
  21.0 2.2 pad_maximum_fusion.2
  23.7 1.7 collective-permute-start.6
  26.0 2.2 bitcast_select_fusion
  28.2 6.5 %collective-permute-done.1.x2 = bf16[512,768]{1,0:T(8,128)(2,1)} collective-permute-done((bf16[512,768]{1,0:T(8,128)(2,1)}, bf16[512,768]{1,0:T(8,128)(2,1)}, u32[]{:S(2)}, u32[]{:S(2)}) %collective-permute-start.1) | collective-permute-done | bytes 786464 | tf_op jit(solution)/shard_map/ppermute | solution.py:637
  34.7 5.5 %collective-permute-start.2 = (bf16[512,768]{1,0:T(8,128)(2,1)}, bf16[512,768]{1,0:T(8,128)(2,1)}, u32[]{:S(2)}, u32[]{:S(2)}) collective-permute-start(bf16[512,768]{1,0:T(8,128)(2,1)} %collective-permute-done.1.x2), channel_id=1, source_target_pairs={{0,4},{4,0},{8,12},{12,8},{1,5},{5,1},{9,13},{13,9},{2,6},{6,2},{1... | collective-permute-start | bytes 2359304 | tf_op jit(solution)/shard_map/ppermute | solution.py:637
  41.5 4.9 %collective-permute-start.5 = (bf16[512,768]{1,0:T(8,128)(2,1)S(1)}, bf16[512,768]{1,0:T(8,128)(2,1)}, u32[]{:S(2)}, u32[]{:S(2)}) collective-permute-start(bf16[512,768]{1,0:T(8,128)(2,1)S(1)} %get-tuple-element.179.c0), channel_id=1, source_target_pairs={{0,8},{4,12},{8,0},{12,4},{1,9},{5,13},{9,1},{13,5},{2,10},{6,14},... | collective-permute-start | bytes 2359304 | tf_op jit(solution)/shard_map/ppermute | solution.py:637
  46.4 1.4 broadcast_select_fusion.8
  49.7 1.4 pad.20
  51.8 1.4 fusion.42
  53.2 13.1 %project.1 = (bf16[2048,768]{1,0:T(8,128)(2,1)}, bf16[2048,384]{1,0:T(8,128)(2,1)}, bf16[2048,384]{1,0:T(8,128)(2,1)}, bf16[2048,384]{1,0:T(8,128)(2,1)}, bf16[3...) custom-call(s32[8]{0:T(128)} %pad_add_fusion.info, ...), custom_call_target="tpu_custom_call" | custom-call | flops 37748736 | tf_op jit(solution)/shard_map/project/pallas_call | solution.py:147
  66.3 2.5 broadcast_select_fusion.3
  69.8 3.2 collective-permute-start.9
  73.0 11.0 %attend.2 = (bf16[1024,192]{1,0:T(8,128)(2,1)}, f32[192,1024]{1,0:T(8,128)}, f32[8,1024]{1,0:T(8,128)}) custom-call(bf16[2048,384]{1,0:T(8,128)(2,1)} %get-tuple-element.184.qa, bf16[2048,384]{1,0:T(8,128)(2,1)} %get-tuple-element.172.ka, bf16[384,2048]{1,0:T(8,128)(2,1)} %get-tuple-element.173.vt, f32[3,3,128,128]{3,2,1,0:T(8,128)} %get-tuple-element.174.near), custom_call_target="tpu_custom_call" | custom-call | flops 125829120 | tf_op jit(solution)/shard_map/attend/pallas_call | solution.py:233
  84.7 1.3 collective-permute-start.12
  86.7 11.5 %attend.3 = (bf16[1024,192]{1,0:T(8,128)(2,1)}, f32[192,1024]{1,0:T(8,128)}, f32[8,1024]{1,0:T(8,128)}) custom-call(bf16[2048,384]{1,0:T(8,128)(2,1)} %get-tuple-element.184.qa, bf16[2048,384]{1,0:T(8,128)(2,1)} %get-tuple-element.172.ka, bf16[384,2048]{1,0:T(8,128)(2,1)} %get-tuple-element.173.vt, f32[3,3,128,128]{3,2,1,0:T(8,128)} %get-tuple-element.174.near), custom_call_target="tpu_custom_call" | custom-call | flops 125829120 | tf_op jit(solution)/shard_map/attend/pallas_call | solution.py:233
  98.3 1.4 collective-permute-done.11.m2
  99.7 9.5 %collective-permute-done.12.m3 = bf16[1024,192]{1,0:T(8,128)(2,1)} collective-permute-done((bf16[1024,192]{1,0:T(8,128)(2,1)}, bf16[1024,192]{1,0:T(8,128)(2,1)}, u32[]{:S(2)}, u32[]{:S(2)}) %collective-permute-start.12) | collective-permute-done | bytes 393248 | tf_op jit(solution)/shard_map/ppermute | solution.py:637
  111.3 1.8 broadcast_select_fusion.1
  113.1 1.6 pad_maximum_fusion.w_ffn
  114.7 20.5 %middle.2 = (bf16[2,256,768]{2,1,0:T(8,128)(2,1)}, bf16[2,256,768]{2,1,0:T(8,128)(2,1)}, bf16[2,256,768]{2,1,0:T(8,128)(2,1)}, bf16[2,256,768]{2,1,0:T(8,128)(2,...) custom-call(s32[8]{0:T(128)} %pad_add_fusion.info, bf16[512,768]{1,0:T(8,128)(2,1)} %get-tuple-element.377.x0, ...), custom_call_target="tpu_custom_call" | custom-call | flops 188743680 | tf_op jit(solution)/shard_map/middle/pallas_call | solution.py:316
  136.2 1.9 collective-permute-done.19
  139.8 21.2 %middle.3 = (bf16[2,256,768]{2,1,0:T(8,128)(2,1)}, bf16[2,256,768]{2,1,0:T(8,128)(2,1)}, bf16[2,256,768]{2,1,0:T(8,128)(2,1)}, bf16[2,256,768]{2,1,0:T(8,128)(2,...) custom-call(s32[8]{0:T(128)} %pad_add_fusion.info, bf16[512,768]{1,0:T(8,128)(2,1)} %get-tuple-element.377.x0, ...), custom_call_target="tpu_custom_call" | custom-call | flops 188743680 | tf_op jit(solution)/shard_map/middle/pallas_call | solution.py:316
  162.0 2.4 collective-permute-done.22
  168.1 1.8 collective-permute-start.25
  174.4 27.8 %attend_back.2 = (bf16[1024,384]{1,0:T(8,128)(2,1)}, f32[2048,384]{1,0:T(8,128)}, f32[2048,384]{1,0:T(8,128)}, f32[3,3,128,128]{3,2,1,0:T(8,128)}, f32[192,768]{1,0:T(8,128)}, /*index=5*/f32[3,16,128]{2,1,0:T(8,128)}) custom-call(s32[8]{0:T(128)} %pad_add_fusion.info, bf16[2048,384]{1,0:T(8,128)(2,1)} %get-tuple-element.184.qa, ...), custom_call_target="tpu_custom_call" | custom-call | flops 251658240 | tf_op jit(solution)/shard_map/attend_back/pallas_call | solution.py:459
  202.2 2.7 collective-permute-done.26
  204.9 2.0 collective-permute-start.28
  206.9 1.6 add_convert_fusion.2.sum_mine
  211.7 3.3 fusion.15
  216.0 27.6 %attend_back.3 = (bf16[1024,384]{1,0:T(8,128)(2,1)}, bf16[2048,384]{1,0:T(8,128)(2,1)}, bf16[2048,384]{1,0:T(8,128)(2,1)}, f32[3,3,128,128]{3,2,1,0:T(8,128)}, f...) custom-call(s32[8]{0:T(128)} %pad_add_fusion.info, bf16[2048,384]{1,0:T(8,128)(2,1)} %get-tuple-element.184.qa, ...), custom_call_target="tpu_custom_call" | custom-call | flops 251658240 | tf_op jit(solution)/shard_map/attend_back/pallas_call | solution.py:459
  243.5 1.4 broadcast_select_fusion.2
  245.0 9.9 %tail.1 = (bf16[4,256,768]{2,1,0:T(8,128)(2,1)}, bf16[4,256,768]{2,1,0:T(8,128)(2,1)}) custom-call(s32[8]{0:T(128)} %pad_add_fusion.info, bf16[1024,384]{1,0:T(8,128)(2,1)} %get-tuple-element.280.dq0, bf16[1024,384]{1,0:T(8,128)(2,1)} %get-tuple-element.281.dq1, bf16[2048,384]{1,0:T(8,128)(2,1)} %get-tuple-element.282.dk, ...), custom_call_target="tpu_custom_call" | custom-call | flops 56623104 | tf_op jit(solution)/shard_map/tail/pallas_call | solution.py:557
  260.9 3.2 bucket_sums.1
  264.1 1.4 select_reduce_fusion.1
  265.5 2.6 add_convert_fusion.1
  268.1 4.8 %collective-permute-start.31 = (bf16[2,256,768]{2,1,0:T(8,128)(2,1)}, bf16[2,256,768]{2,1,0:T(8,128)(2,1)}, u32[]{:S(2)}, u32[]{:S(2)}) collective-permute-start(bf16[2,256,768]{2,1,0:T(8,128)(2,1)} %add_convert_fusion.1), channel_id=1, source_target_pairs={{0,8},{4,12},{8,0},{12,4},{1,9},{5,13},{9,1},{13,5},{2,10},{6,14},... | collective-permute-start | bytes 2359304 | tf_op jit(solution)/shard_map/ppermute | solution.py:637
  277.8 8.4 %weights.1 = bf16[800,768]{1,0:T(8,128)(2,1)} custom-call(bf16[1024,384]{1,0:T(8,128)(2,1)} %get-tuple-element.280.dq0, bf16[1024,384]{1,0:T(8,128)(2,1)} %get-tuple-element.281.dq1, bf16[2048,384]{1,0:T(8,128)(2,1)} %get-tuple-element.282.dk, bf16[2048,384]{1,0:T(8,128)(2,1)} %get-tuple-element.283.dv, bf16[2048,768]{1,0:T(8,128)(2,1)} %get-tuple-element.170.normed, ...), custom_call_target="tpu_custom_call" | custom-call | flops 56623104 | tf_op jit(solution)/shard_map/weights/pallas_call | solution.py:607
  286.2 2.7 add_convert_fusion
  288.9 2.4 collective-permute-done.31
  291.4 2.2 multiply_reduce_fusion.2
  293.9 2.2 fusion.16
  296.1 1.6 fusion.9
  299.9 1.7 collective-permute-start.36
  301.6 1.9 collective-permute-done.36
  303.5 1.7 collective-permute-start.43
  306.7 1.3 collective-permute-start.32
  308.0 1.6 collective-permute-start.33
  309.6 11.8 %collective-permute-done.34 = bf16[800,384]{1,0:T(8,128)(2,1)} collective-permute-done((bf16[800,384]{1,0:T(8,128)(2,1)}, bf16[800,384]{1,0:T(8,128)(2,1)}, u32[]{:S(2)}, u32[]{:S(2)}) %collective-permute-start.34) | collective-permute-done | bytes 614432 | tf_op jit(solution)/shard_map/ppermute | solution.py:691
  321.4 2.0 add_convert_fusion.7
  323.4 12.7 %collective-permute-done.32 = bf16[512,768]{1,0:T(8,128)(2,1)S(1)} collective-permute-done((bf16[512,768]{1,0:T(8,128)(2,1)}, bf16[512,768]{1,0:T(8,128)(2,1)S(1)}, u32[]{:S(2)}, u32[]{:S(2)}) %collective-permute-start.32) | collective-permute-done | bytes 786464 | tf_op jit(solution)/shard_map/ppermute | solution.py:651
  337.1 2.0 convert_add_fusion
  339.1 1.8 collective-permute-start.41
  343.0 16.5 %collective-permute-start.40 = (bf16[800,384]{1,0:T(8,128)(2,1)S(1)}, bf16[800,384]{1,0:T(8,128)(2,1)S(1)}, u32[]{:S(2)}, u32[]{:S(2)}) collective-permute-start(bf16[800,384]{1,0:T(8,128)(2,1)S(1)} %broadcast_select_fusion.5), channel_id=1, source_target_pairs={{0,4},{4,0},{8,12},{12,8},{1,5},{5,1},{9,13},{13,9},{2,6},{6,2},{1... | collective-permute-start | bytes 1843208 | tf_op jit(solution)/shard_map/ppermute | solution.py:637
  360.0 1.4 copy-done.22
  361.7 1.6 pad_maximum_fusion.1
  363.3 8.9 %collective-permute-done.42 = f32[2,768]{1,0:T(2,128)S(1)} collective-permute-done((f32[2,768]{1,0:T(2,128)S(1)}, f32[2,768]{1,0:T(2,128)S(1)}, u32[]{:S(2)}, u32[]{:S(2)}) %collective-permute-start.42) | collective-permute-done | bytes 6176 | tf_op jit(solution)/shard_map/ppermute | solution.py:651
  373.0 1.6 slice_bitcast_fusion
  377.2 11.2 %collective-permute-done.46 = bf16[800,384]{1,0:T(8,128)(2,1)S(1)} collective-permute-done((bf16[800,384]{1,0:T(8,128)(2,1)S(1)}, bf16[800,384]{1,0:T(8,128)(2,1)S(1)}, u32[]{:S(2)}, u32[]{:S(2)}) %collective-permute-start.46) | collective-permute-done | bytes 614432 | tf_op jit(solution)/shard_map/ppermute | solution.py:637
  388.5 8.9 %collective-permute-done.45 = bf16[512,768]{1,0:T(8,128)(2,1)S(1)} collective-permute-done((bf16[512,768]{1,0:T(8,128)(2,1)S(1)}, bf16[512,768]{1,0:T(8,128)(2,1)S(1)}, u32[]{:S(2)}, u32[]{:S(2)}) %collective-permute-start.45) | collective-permute-done | bytes 786464 | tf_op jit(solution)/shard_map/ppermute | solution.py:651
  399.4 1.4 copy.35
  (273 shorter events, 56.3 us)
Async XLA Ops:
  7.2 197.7 %reduce-scatter.2.cloned.1.call-start = ((), (), s32[]{:S(2)}) async-start(), calls=%async_computation.1 | async-start | bytes 3538944 | tf_op jit(solution)/shard_map/reduce_scatter | solution.py:849
  7.3 10.9 %copy-start.34 = (bf16[768,384]{1,0:T(8,128)(2,1)S(1)}, bf16[768,384]{1,0:T(8,128)(2,1)}, u32[]{:S(2)}) copy-start(bf16[768,384]{1,0:T(8,128)(2,1)} %param.22) | copy-start | bytes 1769476
  10.4 8.9 %collective-permute-start.3 = (bf16[800,384]{1,0:T(8,128)(2,1)S(1)}, bf16[800,384]{1,0:T(8,128)(2,1)}, u32[]{:S(2)}, u32[]{:S(2)}) collective-permute-start(bf16[800,384]{1,0:T(8,128)(2,1)S(1)} %concatenate.37), channel_id=1, source_target_pairs={{4,6},{5,7},{6,4},{7,5},{8,9},{9,8},{10,11},{11,10},{12,15},{13,14... | collective-permute-start | bytes 1843208 | tf_op jit(solution)/shard_map/ppermute | solution.py:646
  11.9 22.8 %collective-permute-start.1 = (bf16[512,768]{1,0:T(8,128)(2,1)}, bf16[512,768]{1,0:T(8,128)(2,1)}, u32[]{:S(2)}, u32[]{:S(2)}) collective-permute-start(bf16[512,768]{1,0:T(8,128)(2,1)} %get-tuple-element.377.x0), channel_id=1, source_target_pairs={{0,8},{4,12},{8,0},{12,4},{1,9},{5,13},{9,1},{13,5},{2,10},{6,14},... | collective-permute-start | bytes 2359304 | tf_op jit(solution)/shard_map/ppermute | solution.py:637
  16.9 36.3 %collective-permute-start = (bf16[512,768]{1,0:T(8,128)(2,1)}, bf16[512,768]{1,0:T(8,128)(2,1)}, u32[]{:S(2)}, u32[]{:S(2)}) collective-permute-start(bf16[512,768]{1,0:T(8,128)(2,1)} %get-tuple-element.377.x0), channel_id=1, source_target_pairs={{0,4},{4,0},{8,12},{12,8},{1,5},{5,1},{9,13},{13,9},{2,6},{6,2},{1... | collective-permute-start | bytes 2359304 | tf_op jit(solution)/shard_map/ppermute | solution.py:637
  19.3 8.9 %copy-start.18 = (bf16[800,384]{1,0:T(8,128)(2,1)}, bf16[800,384]{1,0:T(8,128)(2,1)S(1)}, u32[]{:S(2)}) copy-start(bf16[800,384]{1,0:T(8,128)(2,1)S(1)} %broadcast_select_fusion.6) | copy-start | bytes 1843204
  19.4 27.0 %collective-permute-start.4 = (bf16[800,384]{1,0:T(8,128)(2,1)S(1)}, bf16[800,384]{1,0:T(8,128)(2,1)}, u32[]{:S(2)}, u32[]{:S(2)}) collective-permute-start(bf16[800,384]{1,0:T(8,128)(2,1)S(1)} %broadcast_select_fusion.6), channel_id=1, source_target_pairs={{0,16},{16,0},{1,17},{17,1},{2,18},{18,2},{3,19},{19,3},{4,20},{20... | collective-permute-start | bytes 1843208 | tf_op jit(solution)/shard_map/ppermute | solution.py:691
  23.7 42.6 %collective-permute-start.6 = (bf16[384,1536]{1,0:T(8,128)(2,1)}, bf16[384,1536]{1,0:T(8,128)(2,1)}, u32[]{:S(2)}, u32[]{:S(2)}) collective-permute-start(bf16[384,1536]{1,0:T(8,128)(2,1)} %pad_maximum_fusion.2), channel_id=1, source_target_pairs={{4,6},{5,7},{6,4},{7,5},{8,9},{9,8},{10,11},{11,10},{12,15},{13,14... | collective-permute-start | bytes 3538952 | tf_op jit(solution)/shard_map/ppermute | solution.py:646
  28.2 20.4 %copy-start = (bf16[512,768]{1,0:T(8,128)(2,1)}, bf16[512,768]{1,0:T(8,128)(2,1)S(1)}, u32[]{:S(2)}) copy-start(bf16[512,768]{1,0:T(8,128)(2,1)S(1)} %get-tuple-element.179.c0) | copy-start | bytes 2359300
  34.7 18.5 %collective-permute-start.2 = (bf16[512,768]{1,0:T(8,128)(2,1)}, bf16[512,768]{1,0:T(8,128)(2,1)}, u32[]{:S(2)}, u32[]{:S(2)}) collective-permute-start(bf16[512,768]{1,0:T(8,128)(2,1)} %collective-permute-done.1.x2), channel_id=1, source_target_pairs={{0,4},{4,0},{8,12},{12,8},{1,5},{5,1},{9,13},{13,9},{2,6},{6,2},{1... | collective-permute-start | bytes 2359304 | tf_op jit(solution)/shard_map/ppermute | solution.py:637
  41.5 27.2 %collective-permute-start.5 = (bf16[512,768]{1,0:T(8,128)(2,1)S(1)}, bf16[512,768]{1,0:T(8,128)(2,1)}, u32[]{:S(2)}, u32[]{:S(2)}) collective-permute-start(bf16[512,768]{1,0:T(8,128)(2,1)S(1)} %get-tuple-element.179.c0), channel_id=1, source_target_pairs={{0,8},{4,12},{8,0},{12,4},{1,9},{5,13},{9,1},{13,5},{2,10},{6,14},... | collective-permute-start | bytes 2359304 | tf_op jit(solution)/shard_map/ppermute | solution.py:637
  46.4 37.6 %collective-permute-start.7 = (bf16[512,768]{1,0:T(8,128)(2,1)S(1)}, bf16[512,768]{1,0:T(8,128)(2,1)}, u32[]{:S(2)}, u32[]{:S(2)}) collective-permute-start(bf16[512,768]{1,0:T(8,128)(2,1)S(1)} %get-tuple-element.179.c0), channel_id=1, source_target_pairs={{0,4},{4,0},{8,12},{12,8},{1,5},{5,1},{9,13},{13,9},{2,6},{6,2},{1... | collective-permute-start | bytes 2359304 | tf_op jit(solution)/shard_map/ppermute | solution.py:637
  68.7 15.3 %collective-permute-start.8 = (bf16[512,768]{1,0:T(8,128)(2,1)}, bf16[512,768]{1,0:T(8,128)(2,1)}, u32[]{:S(2)}, u32[]{:S(2)}) collective-permute-start(bf16[512,768]{1,0:T(8,128)(2,1)} %collective-permute-done.5.c2), channel_id=1, source_target_pairs={{0,4},{4,0},{8,12},{12,8},{1,5},{5,1},{9,13},{13,9},{2,6},{6,2},{1... | collective-permute-start | bytes 2359304 | tf_op jit(solution)/shard_map/ppermute | solution.py:637
  69.3 39.9 %collective-permute-start.15 = (bf16[384,1536]{1,0:T(8,128)(2,1)}, bf16[384,1536]{1,0:T(8,128)(2,1)}, u32[]{:S(2)}, u32[]{:S(2)}) collective-permute-start(bf16[384,1536]{1,0:T(8,128)(2,1)} %broadcast_select_fusion.3), channel_id=1, source_target_pairs={{0,16},{16,0},{1,17},{17,1},{2,18},{18,2},{3,19},{19,3},{4,20},{20... | collective-permute-start | bytes 3538952 | tf_op jit(solution)/shard_map/ppermute | solution.py:691
  69.8 14.2 %copy-start.13 = (bf16[192,768]{1,0:T(8,128)(2,1)}, bf16[192,768]{1,0:T(8,128)(2,1)S(1)}, u32[]{:S(2)}) copy-start(bf16[192,768]{1,0:T(8,128)(2,1)S(1)} %fusion.29.w0) | copy-start | bytes 884740
  69.8 14.2 %collective-permute-start.9 = (bf16[192,768]{1,0:T(8,128)(2,1)S(1)}, bf16[192,768]{1,0:T(8,128)(2,1)S(1)}, u32[]{:S(2)}, u32[]{:S(2)}) collective-permute-start(bf16[192,768]{1,0:T(8,128)(2,1)S(1)} %fusion.29.w0), channel_id=1, source_target_pairs={{0,8},{4,12},{8,0},{12,4},{1,9},{5,13},{9,1},{13,5},{2,10},{6,14},... | collective-permute-start | bytes 884744 | tf_op jit(solution)/shard_map/ppermute | solution.py:637
  73.0 13.1 %collective-permute-start.13 = (bf16[192,768]{1,0:T(8,128)(2,1)S(1)}, bf16[192,768]{1,0:T(8,128)(2,1)S(1)}, u32[]{:S(2)}, u32[]{:S(2)}) collective-permute-start(bf16[192,768]{1,0:T(8,128)(2,1)S(1)} %fusion.29.w0), channel_id=1, source_target_pairs={{0,4},{4,0},{8,12},{12,8},{1,5},{5,1},{9,13},{13,9},{2,6},{6,2},{1... | collective-permute-start | bytes 884744 | tf_op jit(solution)/shard_map/ppermute | solution.py:637
  84.0 14.2 %copy-start.23 = (bf16[192,768]{1,0:T(8,128)(2,1)}, bf16[192,768]{1,0:T(8,128)(2,1)S(1)}, u32[]{:S(2)}) copy-start(bf16[192,768]{1,0:T(8,128)(2,1)S(1)} %collective-permute-done.9.w2) | copy-start | bytes 884740
  84.0 14.2 %collective-permute-start.10 = (bf16[1024,192]{1,0:T(8,128)(2,1)}, bf16[1024,192]{1,0:T(8,128)(2,1)S(1)}, u32[]{:S(2)}, u32[]{:S(2)}) collective-permute-start(bf16[1024,192]{1,0:T(8,128)(2,1)} %get-tuple-element.190.m0), channel_id=1, source_target_pairs={{0,4},{4,0},{8,12},{12,8},{1,5},{5,1},{9,13},{13,9},{2,6},{6,2},{1... | collective-permute-start | bytes 1179656 | tf_op jit(solution)/shard_map/ppermute | solution.py:637
  84.6 15.1 %collective-permute-start.11 = (bf16[1024,192]{1,0:T(8,128)(2,1)}, bf16[1024,192]{1,0:T(8,128)(2,1)}, u32[]{:S(2)}, u32[]{:S(2)}) collective-permute-start(bf16[1024,192]{1,0:T(8,128)(2,1)} %get-tuple-element.190.m0), channel_id=1, source_target_pairs={{0,8},{4,12},{8,0},{12,4},{1,9},{5,13},{9,1},{13,5},{2,10},{6,14},... | collective-permute-start | bytes 1179656 | tf_op jit(solution)/shard_map/ppermute | solution.py:637
  84.7 24.5 %collective-permute-start.12 = (bf16[1024,192]{1,0:T(8,128)(2,1)}, bf16[1024,192]{1,0:T(8,128)(2,1)}, u32[]{:S(2)}, u32[]{:S(2)}) collective-permute-start(bf16[1024,192]{1,0:T(8,128)(2,1)} %get-tuple-element.190.m0), channel_id=1, source_target_pairs={{0,12},{4,8},{8,4},{12,0},{1,13},{5,9},{9,5},{13,1},{2,14},{6,10},... | collective-permute-start | bytes 1179656 | tf_op jit(solution)/shard_map/ppermute | solution.py:637
  86.0 12.2 %copy-start.24 = (bf16[192,768]{1,0:T(8,128)(2,1)}, bf16[192,768]{1,0:T(8,128)(2,1)S(1)}, u32[]{:S(2)}) copy-start(bf16[192,768]{1,0:T(8,128)(2,1)S(1)} %collective-permute-done.13.w1) | copy-start | bytes 884740
  86.0 12.2 %collective-permute-start.14 = (bf16[192,768]{1,0:T(8,128)(2,1)S(1)}, bf16[192,768]{1,0:T(8,128)(2,1)S(1)}, u32[]{:S(2)}, u32[]{:S(2)}) collective-permute-start(bf16[192,768]{1,0:T(8,128)(2,1)S(1)} %collective-permute-done.9.w2), channel_id=1, source_target_pairs={{0,4},{4,0},{8,12},{12,8},{1,5},{5,1},{9,13},{13,9},{2,6},{6,2},{1... | collective-permute-start | bytes 884744 | tf_op jit(solution)/shard_map/ppermute | solution.py:637
  98.3 14.8 %copy-start.25 = (bf16[192,768]{1,0:T(8,128)(2,1)}, bf16[192,768]{1,0:T(8,128)(2,1)S(1)}, u32[]{:S(2)}) copy-start(bf16[192,768]{1,0:T(8,128)(2,1)S(1)} %collective-permute-done.14.w3) | copy-start | bytes 884740
  98.3 10.9 %copy-start.38 = (bf16[1024,192]{1,0:T(8,128)(2,1)}, bf16[1024,192]{1,0:T(8,128)(2,1)S(1)}, u32[]{:S(2)}) copy-start(bf16[1024,192]{1,0:T(8,128)(2,1)S(1)} %collective-permute-done.10.m1) | copy-start | bytes 1179652
  109.2 26.0 %collective-permute-start.16 = (bf16[1024,192]{1,0:T(8,128)(2,1)}, bf16[1024,192]{1,0:T(8,128)(2,1)S(1)}, u32[]{:S(2)}, u32[]{:S(2)}) collective-permute-start(bf16[1024,192]{1,0:T(8,128)(2,1)} %get-tuple-element.214.m0), channel_id=1, source_target_pairs={{0,4},{4,0},{8,12},{12,8},{1,5},{5,1},{9,13},{13,9},{2,6},{6,2},{1... | collective-permute-start | bytes 1179656 | tf_op jit(solution)/shard_map/ppermute | solution.py:637
  109.9 25.3 %collective-permute-start.17 = (bf16[1024,192]{1,0:T(8,128)(2,1)}, bf16[1024,192]{1,0:T(8,128)(2,1)S(1)}, u32[]{:S(2)}, u32[]{:S(2)}) collective-permute-start(bf16[1024,192]{1,0:T(8,128)(2,1)} %get-tuple-element.214.m0), channel_id=1, source_target_pairs={{0,8},{4,12},{8,0},{12,4},{1,9},{5,13},{9,1},{13,5},{2,10},{6,14},... | collective-permute-start | bytes 1179656 | tf_op jit(solution)/shard_map/ppermute | solution.py:637
  110.2 25.0 %collective-permute-start.18 = (bf16[1024,192]{1,0:T(8,128)(2,1)}, bf16[1024,192]{1,0:T(8,128)(2,1)S(1)}, u32[]{:S(2)}, u32[]{:S(2)}) collective-permute-start(bf16[1024,192]{1,0:T(8,128)(2,1)} %get-tuple-element.214.m0), channel_id=1, source_target_pairs={{0,12},{4,8},{8,4},{12,0},{1,13},{5,9},{9,5},{13,1},{2,14},{6,10},... | collective-permute-start | bytes 1179656 | tf_op jit(solution)/shard_map/ppermute | solution.py:637
  135.2 2.9 collective-permute-start.19
  139.4 21.6 %collective-permute-start.20 = (bf16[2,256,768]{2,1,0:T(8,128)(2,1)S(1)}, bf16[2,256,768]{2,1,0:T(8,128)(2,1)S(1)}, u32[]{:S(2)}, u32[]{:S(2)}) collective-permute-start(bf16[2,256,768]{2,1,0:T(8,128)(2,1)S(1)} %add_convert_fusion.5), channel_id=1, source_target_pairs={{0,8},{4,12},{8,0},{12,4},{1,9},{5,13},{9,1},{13,5},{2,10},{6,14},... | collective-permute-start | bytes 2359304 | tf_op jit(solution)/shard_map/ppermute | solution.py:637
  161.9 2.5 collective-permute-start.22
  165.7 170.4 %all-gather.3.cloned.1.call-start = ((), (), s32[]{:S(2)}) async-start(), calls=%async_computation.2 | async-start | bytes 3932160 | tf_op jit(solution)/shard_map/all_gather | solution.py:874
  166.0 3.9 collective-permute-start.23
  166.2 4.0 collective-permute-start.24
  167.9 5.6 %collective-permute-start.21 = (bf16[2,256,768]{2,1,0:T(8,128)(2,1)S(1)}, bf16[2,256,768]{2,1,0:T(8,128)(2,1)S(1)}, u32[]{:S(2)}, u32[]{:S(2)}) collective-permute-start(bf16[2,256,768]{2,1,0:T(8,128)(2,1)S(1)} %add_convert_fusion.4.sum_mine), channel_id=1, source_target_pairs={{0,4},{4,0},{8,12},{12,8},{1,5},{5,1},{9,13},{13,9},{2,6},{6,2},{1... | collective-permute-start | bytes 2359304 | tf_op jit(solution)/shard_map/ppermute | solution.py:637
  168.1 34.1 %collective-permute-start.25 = (bf16[2,256,768]{2,1,0:T(8,128)(2,1)S(1)}, bf16[2,256,768]{2,1,0:T(8,128)(2,1)}, u32[]{:S(2)}, u32[]{:S(2)}) collective-permute-start(bf16[2,256,768]{2,1,0:T(8,128)(2,1)S(1)} %add_convert_fusion.3), channel_id=1, source_target_pairs={{0,8},{4,12},{8,0},{12,4},{1,9},{5,13},{9,1},{13,5},{2,10},{6,14},... | collective-permute-start | bytes 2359304 | tf_op jit(solution)/shard_map/ppermute | solution.py:637
  172.2 32.7 %collective-permute-start.26 = (bf16[2,256,768]{2,1,0:T(8,128)(2,1)}, bf16[2,256,768]{2,1,0:T(8,128)(2,1)}, u32[]{:S(2)}, u32[]{:S(2)}) collective-permute-start(bf16[2,256,768]{2,1,0:T(8,128)(2,1)} %pad_maximum_fusion.3), channel_id=1, source_target_pairs={{0,8},{4,12},{8,0},{12,4},{1,9},{5,13},{9,1},{13,5},{2,10},{6,14},... | collective-permute-start | bytes 2359304 | tf_op jit(solution)/shard_map/ppermute | solution.py:637
  204.9 38.6 %collective-permute-start.28 = (bf16[384,1536]{1,0:T(8,128)(2,1)}, bf16[384,1536]{1,0:T(8,128)(2,1)}, u32[]{:S(2)}, u32[]{:S(2)}) collective-permute-start(bf16[384,1536]{1,0:T(8,128)(2,1)} %reduce-scatter.2.cloned.1.call-done), channel_id=1, source_target_pairs={{4,6},{6,4},{7,5},{8,9},{10,11},{11,10},{12,15},{14,13},{15,12},{2... | collective-permute-start | bytes 3538952 | tf_op jit(solution)/shard_map/ppermute | solution.py:646
  208.5 7.5 %collective-permute-start.27 = (bf16[2,256,768]{2,1,0:T(8,128)(2,1)S(1)}, bf16[2,256,768]{2,1,0:T(8,128)(2,1)}, u32[]{:S(2)}, u32[]{:S(2)}) collective-permute-start(bf16[2,256,768]{2,1,0:T(8,128)(2,1)S(1)} %add_convert_fusion.2.sum_mine), channel_id=1, source_target_pairs={{0,4},{4,0},{8,12},{12,8},{1,5},{5,1},{9,13},{13,9},{2,6},{6,2},{1... | collective-permute-start | bytes 2359304 | tf_op jit(solution)/shard_map/ppermute | solution.py:637
  254.9 10.7 %collective-permute-start.29 = (bf16[4,256,768]{2,1,0:T(8,128)(2,1)}, bf16[4,256,768]{2,1,0:T(8,128)(2,1)}, u32[]{:S(2)}, u32[]{:S(2)}) collective-permute-start(bf16[4,256,768]{2,1,0:T(8,128)(2,1)} %get-tuple-element.274), channel_id=1, source_target_pairs={{0,4},{4,0},{8,12},{12,8},{1,5},{5,1},{9,13},{13,9},{2,6},{6,2},{1... | collective-permute-start | bytes 4718600 | tf_op jit(solution)/shard_map/ppermute | solution.py:637
  255.6 10.0 %collective-permute-start.30 = (bf16[384,1536]{1,0:T(8,128)(2,1)S(1)}, bf16[384,1536]{1,0:T(8,128)(2,1)}, u32[]{:S(2)}, u32[]{:S(2)}) collective-permute-start(bf16[384,1536]{1,0:T(8,128)(2,1)S(1)} %broadcast_select_fusion.2), channel_id=1, source_target_pairs={{0,4},{4,0},{8,12},{12,8},{1,5},{5,1},{9,13},{13,9},{2,6},{6,2},{1... | collective-permute-start | bytes 3538952 | tf_op jit(solution)/shard_map/ppermute | solution.py:637
  265.5 8.3 %copy-start.51 = (f32[3]{0:T(128)S(1)}, f32[3]{0:T(128)}, u32[]{:S(2)}) copy-start(f32[3]{0:T(128)} %get-tuple-element.358) | copy-start | bytes 40
  268.1 23.2 %collective-permute-start.31 = (bf16[2,256,768]{2,1,0:T(8,128)(2,1)}, bf16[2,256,768]{2,1,0:T(8,128)(2,1)}, u32[]{:S(2)}, u32[]{:S(2)}) collective-permute-start(bf16[2,256,768]{2,1,0:T(8,128)(2,1)} %add_convert_fusion.1), channel_id=1, source_target_pairs={{0,8},{4,12},{8,0},{12,4},{1,9},{5,13},{9,1},{13,5},{2,10},{6,14},... | collective-permute-start | bytes 2359304 | tf_op jit(solution)/shard_map/ppermute | solution.py:637
  286.2 7.4 %copy-start.8 = (f32[2,256,768]{2,1,0:T(8,128)S(1)}, f32[2,256,768]{2,1,0:T(8,128)}, u32[]{:S(2)}) copy-start(f32[2,256,768]{2,1,0:T(8,128)} %select_convert_fusion) | copy-start | bytes 4718596
  297.8 7.5 %copy-start.9 = (bf16[800,768]{1,0:T(8,128)(2,1)S(1)}, bf16[800,768]{1,0:T(8,128)(2,1)}, u32[]{:S(2)}) copy-start(bf16[800,768]{1,0:T(8,128)(2,1)} %weights.1) | copy-start | bytes 3686404
  298.7 1.2 collective-permute-start.35
  299.9 3.6 collective-permute-start.36
  303.5 33.5 %collective-permute-start.43 = (bf16[384,1536]{1,0:T(8,128)(2,1)}, bf16[384,1536]{1,0:T(8,128)(2,1)}, u32[]{:S(2)}, u32[]{:S(2)}) collective-permute-start(bf16[384,1536]{1,0:T(8,128)(2,1)} %add_convert_fusion), channel_id=1, source_target_pairs={{0,8},{4,12},{8,0},{12,4},{1,9},{5,13},{9,1},{13,5},{2,10},{6,14},... | collective-permute-start | bytes 3538952 | tf_op jit(solution)/shard_map/ppermute | solution.py:637
  306.2 15.2 %collective-permute-start.34 = (bf16[800,384]{1,0:T(8,128)(2,1)}, bf16[800,384]{1,0:T(8,128)(2,1)}, u32[]{:S(2)}, u32[]{:S(2)}) collective-permute-start(bf16[800,384]{1,0:T(8,128)(2,1)} %constant_dynamic-slice_fusion.1), channel_id=1, source_target_pairs={{0,16},{16,0},{1,17},{17,1},{2,18},{18,2},{3,19},{19,3},{4,20},{20... | collective-permute-start | bytes 1843208 | tf_op jit(solution)/shard_map/ppermute | solution.py:691
  306.7 29.4 %collective-permute-start.32 = (bf16[512,768]{1,0:T(8,128)(2,1)}, bf16[512,768]{1,0:T(8,128)(2,1)S(1)}, u32[]{:S(2)}, u32[]{:S(2)}) collective-permute-start(bf16[512,768]{1,0:T(8,128)(2,1)} %pad_maximum_fusion.5), channel_id=1, source_target_pairs={{0,1},{2,3},{4,5},{6,7},{8,9},{10,11},{12,13},{14,15},{16,17},{18,... | collective-permute-start | bytes 2359304 | tf_op jit(solution)/shard_map/ppermute | solution.py:651
  308.0 28.1 %collective-permute-start.33 = (bf16[512,768]{1,0:T(8,128)(2,1)}, bf16[512,768]{1,0:T(8,128)(2,1)}, u32[]{:S(2)}, u32[]{:S(2)}) collective-permute-start(bf16[512,768]{1,0:T(8,128)(2,1)} %pad_maximum_fusion.5), channel_id=1, source_target_pairs={{3,2},{2,1},{7,6},{6,5},{11,10},{10,9},{15,14},{14,13},{19,18},{18... | collective-permute-start | bytes 2359304 | tf_op jit(solution)/shard_map/ppermute | solution.py:651
  336.1 6.8 %collective-permute-start.39 = (bf16[800,384]{1,0:T(8,128)(2,1)}, bf16[800,384]{1,0:T(8,128)(2,1)S(1)}, u32[]{:S(2)}, u32[]{:S(2)}) collective-permute-start(bf16[800,384]{1,0:T(8,128)(2,1)} %add_convert_fusion.7), channel_id=1, source_target_pairs={{4,6},{6,4},{7,5},{8,9},{10,11},{11,10},{12,15},{14,13},{15,12},{2... | collective-permute-start | bytes 1843208 | tf_op jit(solution)/shard_map/ppermute | solution.py:646
  339.1 22.5 %collective-permute-start.41 = (f32[2,768]{1,0:T(2,128)S(1)}, f32[2,768]{1,0:T(2,128)S(1)}, u32[]{:S(2)}, u32[]{:S(2)}) collective-permute-start(f32[2,768]{1,0:T(2,128)S(1)} %add.384), channel_id=1, source_target_pairs={{0,16},{16,0},{1,17},{17,1},{2,18},{18,2},{3,19},{19,3},{4,20},{20... | collective-permute-start | bytes 18440 | tf_op jit(solution)/shard_map/ppermute | solution.py:691
  340.9 31.5 %collective-permute-start.37 = (bf16[512,768]{1,0:T(8,128)(2,1)S(1)}, bf16[512,768]{1,0:T(8,128)(2,1)S(1)}, u32[]{:S(2)}, u32[]{:S(2)}) collective-permute-start(bf16[512,768]{1,0:T(8,128)(2,1)S(1)} %collective-permute-done.32), channel_id=1, source_target_pairs={{1,2},{5,6},{9,10},{13,14},{17,18},{21,22},{25,26},{29,30}} | collective-permute-start | bytes 2359304 | tf_op jit(solution)/shard_map/ppermute | solution.py:651
  341.6 30.8 %collective-permute-start.38 = (bf16[512,768]{1,0:T(8,128)(2,1)}, bf16[512,768]{1,0:T(8,128)(2,1)S(1)}, u32[]{:S(2)}, u32[]{:S(2)}) collective-permute-start(bf16[512,768]{1,0:T(8,128)(2,1)} %collective-permute-done.33), channel_id=1, source_target_pairs={{2,1},{1,0},{6,5},{5,4},{10,9},{9,8},{14,13},{13,12},{18,17},{17,1... | collective-permute-start | bytes 2359304 | tf_op jit(solution)/shard_map/ppermute | solution.py:651
  343.0 29.2 %collective-permute-start.40 = (bf16[800,384]{1,0:T(8,128)(2,1)S(1)}, bf16[800,384]{1,0:T(8,128)(2,1)S(1)}, u32[]{:S(2)}, u32[]{:S(2)}) collective-permute-start(bf16[800,384]{1,0:T(8,128)(2,1)S(1)} %broadcast_select_fusion.5), channel_id=1, source_target_pairs={{0,4},{4,0},{8,12},{12,8},{1,5},{5,1},{9,13},{13,9},{2,6},{6,2},{1... | collective-permute-start | bytes 1843208 | tf_op jit(solution)/shard_map/ppermute | solution.py:637
  361.6 10.6 %collective-permute-start.42 = (f32[2,768]{1,0:T(2,128)S(1)}, f32[2,768]{1,0:T(2,128)S(1)}, u32[]{:S(2)}, u32[]{:S(2)}) collective-permute-start(f32[2,768]{1,0:T(2,128)S(1)} %add.386), channel_id=1, source_target_pairs={{0,1},{1,0},{2,3},{3,2},{4,5},{5,4},{6,7},{7,6},{8,9},{9,8},{10,11... | collective-permute-start | bytes 18440 | tf_op jit(solution)/shard_map/ppermute | solution.py:651
  372.4 4.8 %collective-permute-start.47 = (f32[2,768]{1,0:T(2,128)S(1)}, f32[2,768]{1,0:T(2,128)S(1)}, u32[]{:S(2)}, u32[]{:S(2)}) collective-permute-start(f32[2,768]{1,0:T(2,128)S(1)} %add.387), channel_id=1, source_target_pairs={{0,2},{1,3},{2,0},{3,1},{4,6},{5,7},{6,4},{7,5},{8,10},{9,11},{10,... | collective-permute-start | bytes 18440 | tf_op jit(solution)/shard_map/ppermute | solution.py:651
  372.5 15.9 %collective-permute-start.46 = (bf16[800,384]{1,0:T(8,128)(2,1)S(1)}, bf16[800,384]{1,0:T(8,128)(2,1)S(1)}, u32[]{:S(2)}, u32[]{:S(2)}) collective-permute-start(bf16[800,384]{1,0:T(8,128)(2,1)S(1)} %add_convert_fusion.6), channel_id=1, source_target_pairs={{0,8},{4,12},{8,0},{12,4},{1,9},{5,13},{9,1},{13,5},{2,10},{6,14},... | collective-permute-start | bytes 1843208 | tf_op jit(solution)/shard_map/ppermute | solution.py:637
  374.5 14.0 %collective-permute-start.44 = (bf16[512,768]{1,0:T(8,128)(2,1)S(1)}, bf16[512,768]{1,0:T(8,128)(2,1)S(1)}, u32[]{:S(2)}, u32[]{:S(2)}) collective-permute-start(bf16[512,768]{1,0:T(8,128)(2,1)S(1)} %collective-permute-done.37), channel_id=1, source_target_pairs={{2,3},{6,7},{10,11},{14,15},{18,19},{22,23},{26,27},{30,31}} | collective-permute-start | bytes 2359304 | tf_op jit(solution)/shard_map/ppermute | solution.py:651
  375.2 22.2 %collective-permute-start.45 = (bf16[512,768]{1,0:T(8,128)(2,1)S(1)}, bf16[512,768]{1,0:T(8,128)(2,1)S(1)}, u32[]{:S(2)}, u32[]{:S(2)}) collective-permute-start(bf16[512,768]{1,0:T(8,128)(2,1)S(1)} %collective-permute-done.38), channel_id=1, source_target_pairs={{1,0},{5,4},{9,8},{13,12},{17,16},{21,20},{25,24},{29,28}} | collective-permute-start | bytes 2359304 | tf_op jit(solution)/shard_map/ppermute | solution.py:651
  377.1 22.2 %copy-start.20 = (bf16[3,512,768]{2,1,0:T(8,128)(2,1)}, bf16[3,512,768]{2,1,0:T(8,128)(2,1)S(1)}, u32[]{:S(2)}) copy-start(bf16[3,512,768]{2,1,0:T(8,128)(2,1)S(1)} %bitcast_dynamic-update-slice_fusion.2) | copy-start | bytes 7077892
  388.5 10.9 %copy-start.12 = (f32[768,384]{0,1:T(8,128)S(1)}, f32[768,384]{0,1:T(8,128)}, u32[]{:S(2)}) copy-start(f32[768,384]{0,1:T(8,128)} %get-tuple-element.347) | copy-start | bytes 3538948
  388.5 9.8 %copy-start.31 = (bf16[512,768]{1,0:T(8,128)(2,1)}, bf16[512,768]{1,0:T(8,128)(2,1)S(1)}, u32[]{:S(2)}) copy-start(bf16[512,768]{1,0:T(8,128)(2,1)S(1)} %collective-permute-done.44) | copy-start | bytes 2359300
  (44 other events, 117.2 us)
Sparse Core Ops, SparseCore 0:
  165.9 35.6 reduce-scatter.1
  258.0 72.4 all-gather.2
